TPU v7x, 32 devices: a whole 2x2x4 slice. The times are simulated.
32 devices in a mesh: pair: 2 (over y), dp: 16 (over z, x, core).
Axes of the slice: x: 2, y: 2, z: 4, core: 2. Of those that a mesh axis runs over, the one named last changes fastest.
Arguments:
- tokens: bfloat16 [2, 16384, 768], P('pair', 'dp'), may hold values from -6 to 6
- attend_weight: bfloat16 [2, 768, 2304], P('pair'), may hold values from -0.21875 to 0.21875
- attend_bias: float32 [2, 1536], P('pair'), may hold values from -1.2 to 1.2
- merge_weight: bfloat16 [2, 768, 768], P('pair'), may hold values from -0.625 to 0.625
- merge_bias: float32 [2, 768], P('pair'), may hold values from -1.2 to 1.2
- first_gain: float32 [2, 768], P('pair'), may hold values from 0.5 to 1.5
- first_shift: float32 [2, 768], P('pair'), may hold values from -1.2 to 1.2
- expand_weight: bfloat16 [2, 768, 3072], P('pair'), may hold values from -0.21875 to 0.21875
- expand_bias: float32 [2, 3072], P('pair'), may hold values from -1.2 to 1.2
- reduce_weight: bfloat16 [2, 3072, 768], P('pair'), may hold values from -0.109375 to 0.109375
- reduce_bias: float32 [2, 768], P('pair'), may hold values from -1.2 to 1.2
- second_gain: float32 [2, 768], P('pair'), may hold values from 0.5 to 1.5
- second_shift: float32 [2, 768], P('pair'), may hold values from -1.2 to 1.2
- cotangent: bfloat16 [2, 16384, 768], P('pair', 'dp'), may hold values from -6 to 6
- positives: int32 [256, 4], replicated, may hold values from 0 to 63, as said below
- counts: int32 [256], replicated, may hold values from 1 to 4, as said below
Outputs:
- activations: bfloat16 [2, 16384, 768], P('pair', 'dp')
- contrastive_loss: float32 [], replicated
- input_grad: bfloat16 [2, 16384, 768], P('pair', 'dp')
- attend_weight_grad: float32 [2, 768, 2304], P('pair', 'dp')
- attend_bias_grad: float32 [2, 1536], P('pair', 'dp')
- merge_weight_grad: float32 [2, 768, 768], P('pair', 'dp')
- merge_bias_grad: float32 [2, 768], P('pair', 'dp')
- first_gain_grad: float32 [2, 768], P('pair', 'dp')
- first_shift_grad: float32 [2, 768], P('pair', 'dp')
- expand_weight_grad: float32 [2, 768, 3072], P('pair', 'dp')
- expand_bias_grad: float32 [2, 3072], P('pair', 'dp')
- reduce_weight_grad: float32 [2, 3072, 768], P('pair', 'dp')
- reduce_bias_grad: float32 [2, 768], P('pair', 'dp')
- second_gain_grad: float32 [2, 768], P('pair', 'dp')
- second_shift_grad: float32 [2, 768], P('pair', 'dp')
Inputs may be any that keep to these rules, and one draw needn't show every extreme that they name: `positives`: entries 0 to counts[i] - 1 of row i are the positive passages of question i (passage j is the j-th sequence of tokens[1]); the 4 entries of a row are distinct passages; the other entries are padding. `counts`: some question has 4 positives.
All inputs are finite; a program needn't handle non-finite values.
Results may differ from a plain program's by a relative error of at most 0.012.
Values may be sent and summed in bfloat16 or wider, within the bound.
A program may use at most 192 MiB of HBM per device.

v0:
```python
from functools import partial
import math

import jax
import jax.numpy as jnp
from jax import lax
from jax.sharding import PartitionSpec as P

D = 768
HEADS = 12
HEAD = 64
QLEN = 64
PLEN = 256
BLOCK = 512
KPOS = 4


eps = 1e-06
loss_weight = 32.0
negative = -1e30


def layer_norm(values, scale_gain, shift_row):
    centred = values - jnp.mean(values, axis=-1, keepdims=True)
    inverse = lax.rsqrt(jnp.mean(centred * centred, axis=-1, keepdims=True) + eps)
    normed = centred * inverse
    return (normed * scale_gain + shift_row, normed, inverse)


def norm_backward(upstream, normed, inverse, scale_gain):
    scaled = upstream * scale_gain
    centred = (
        scaled
        - jnp.mean(scaled, axis=-1, keepdims=True)
        - normed * jnp.mean(scaled * normed, axis=-1, keepdims=True)
    )
    return (centred * inverse, jnp.sum(upstream * normed, axis=0), jnp.sum(upstream, axis=0))


def masked_scores(query_block, key_block, same_sequence):
    raw_scores = jnp.einsum(
        "qhd,khd->hqk", query_block, key_block, preferred_element_type=jnp.float32
    ) * (1.0 / math.sqrt(HEAD))
    return jnp.where(same_sequence[None], raw_scores, negative)


def shards(
    tokens,
    attend_weight,
    attend_bias,
    merge_weight,
    merge_bias,
    first_gain,
    first_shift,
    expand_weight,
    expand_bias,
    reduce_weight,
    reduce_bias,
    second_gain,
    second_shift,
    cotangent,
    positives,
    counts,
):
    half_index = lax.axis_index("pair")
    group_index = lax.axis_index("dp")
    span_length = jnp.where(half_index == 0, QLEN, PLEN).astype(jnp.int32)
    token_rows = tokens[0]
    row_count, model_width = token_rows.shape
    block_count = row_count // BLOCK
    places = jnp.arange(BLOCK, dtype=jnp.int32) // span_length
    same_sequence = places[:, None] == places[None, :]
    zero_keys = jnp.zeros((model_width,), jnp.float32)
    full_bias = jnp.concatenate(
        [attend_bias[0, :model_width], zero_keys, attend_bias[0, model_width:]]
    )
    packed = (
        jnp.dot(token_rows, attend_weight[0], preferred_element_type=jnp.float32) + full_bias
    ).astype(jnp.bfloat16)
    heads_split = packed.reshape(block_count, BLOCK, 3, HEADS, HEAD)
    queries = heads_split[:, :, 0]
    keys_all = heads_split[:, :, 1]
    values_all = heads_split[:, :, 2]

    def attend_block(members):
        query_block, key_block, value_block = members
        scores = masked_scores(query_block, key_block, same_sequence)
        peak = jnp.max(scores, axis=-1, keepdims=True)
        totals = jnp.sum(jnp.exp(scores - peak), axis=-1, keepdims=True)
        log_total = peak + jnp.log(totals)
        probs16 = jnp.exp(scores - log_total).astype(jnp.bfloat16)
        mixed = jnp.einsum("hqk,khd->qhd", probs16, value_block, preferred_element_type=jnp.float32)
        return (mixed, log_total[..., 0])

    attended, log_totals = lax.map(attend_block, (queries, keys_all, values_all))
    attended16 = attended.reshape(row_count, model_width).astype(jnp.bfloat16)
    branch = (
        jnp.dot(attended16, merge_weight[0], preferred_element_type=jnp.float32) + merge_bias[0]
    )
    rows_float = token_rows.astype(jnp.float32)
    normed_first, first_normed, first_inverse = layer_norm(
        rows_float + branch, first_gain[0], first_shift[0]
    )
    first16 = normed_first.astype(jnp.bfloat16)
    inner_pre = (
        jnp.dot(first16, expand_weight[0], preferred_element_type=jnp.float32) + expand_bias[0]
    )
    hidden16 = jax.nn.gelu(inner_pre, approximate=False).astype(jnp.bfloat16)
    second = (
        jnp.dot(hidden16, reduce_weight[0], preferred_element_type=jnp.float32) + reduce_bias[0]
    )
    final, final_normed, final_inverse = layer_norm(
        normed_first + second, second_gain[0], second_shift[0]
    )
    question_count = row_count // QLEN
    passage_count = row_count // PLEN
    leading = final.reshape(question_count, QLEN, model_width)[:, 0].astype(jnp.bfloat16)
    every_leading = lax.all_gather(leading, ("pair", "dp"), axis=0, tiled=True)
    half_rows = every_leading.shape[0] // 2
    question_cls = every_leading[:half_rows]
    passage_cls = every_leading[half_rows:].reshape(-1, PLEN // QLEN, model_width)[:, 0]
    root_width = math.sqrt(D)
    match_scores = (
        jnp.einsum("qd,pd->qp", question_cls, passage_cls, preferred_element_type=jnp.float32)
        / root_width
    )
    row_peak = jnp.max(match_scores, axis=1, keepdims=True)
    lse_all = row_peak + jnp.log(jnp.sum(jnp.exp(match_scores - row_peak), axis=1, keepdims=True))
    picked = jnp.take_along_axis(match_scores, positives, axis=1)
    live_slots = jnp.arange(KPOS, dtype=jnp.int32)[None, :] < counts[:, None]
    live_peak = jnp.max(jnp.where(live_slots, picked, negative), axis=1, keepdims=True)
    live_total = jnp.sum(
        jnp.where(live_slots, jnp.exp(picked - live_peak), 0.0), axis=1, keepdims=True
    )
    lse_live = live_peak + jnp.log(live_total)
    loss_value = jnp.mean(lse_all[:, 0] - lse_live[:, 0])
    live_weights = jnp.where(live_slots, jnp.exp(picked - lse_live), 0.0)
    columns = jnp.arange(match_scores.shape[1], dtype=jnp.int32)[None, :]
    grad_match = jnp.exp(match_scores - lse_all)
    for slot in range(KPOS):
        grad_match = grad_match - jnp.where(
            columns == positives[:, slot : slot + 1], live_weights[:, slot : slot + 1], 0.0
        )
    grad_match16 = (loss_weight * grad_match).astype(jnp.bfloat16)
    own_questions = lax.dynamic_slice_in_dim(
        grad_match16, group_index * question_count, question_count, 0
    )
    grad_question = (
        jnp.dot(own_questions, passage_cls, preferred_element_type=jnp.float32) / root_width
    )
    own_passages = lax.dynamic_slice_in_dim(
        grad_match16, group_index * passage_count, passage_count, 1
    )
    grad_passage = (
        jnp.einsum("qp,qd->pd", own_passages, question_cls, preferred_element_type=jnp.float32)
        / root_width
    )
    spread_question = (
        jnp.zeros((question_count, QLEN, model_width), jnp.float32)
        .at[:, 0]
        .set(grad_question)
        .reshape(row_count, model_width)
    )
    spread_passage = (
        jnp.zeros((passage_count, PLEN, model_width), jnp.float32)
        .at[:, 0]
        .set(grad_passage)
        .reshape(row_count, model_width)
    )
    grad_final = cotangent[0].astype(jnp.float32) + jnp.where(
        half_index == 0, spread_question, spread_passage
    )
    grad_pair_two, second_gain_grad, second_shift_grad = norm_backward(
        grad_final, final_normed, final_inverse, second_gain[0]
    )
    grad_second16 = grad_pair_two.astype(jnp.bfloat16)
    reduce_weight_grad = jnp.einsum(
        "tf,td->fd", hidden16, grad_second16, preferred_element_type=jnp.float32
    )
    reduce_bias_grad = jnp.sum(grad_second16.astype(jnp.float32), axis=0)
    grad_hidden = jnp.einsum(
        "td,fd->tf", grad_second16, reduce_weight[0], preferred_element_type=jnp.float32
    )
    _, gelu_pullback = jax.vjp(partial(jax.nn.gelu, approximate=False), inner_pre)
    grad_inner16 = gelu_pullback(grad_hidden)[0].astype(jnp.bfloat16)
    expand_weight_grad = jnp.einsum(
        "td,tf->df", first16, grad_inner16, preferred_element_type=jnp.float32
    )
    expand_bias_grad = jnp.sum(grad_inner16.astype(jnp.float32), axis=0)
    grad_first = (
        jnp.einsum("tf,df->td", grad_inner16, expand_weight[0], preferred_element_type=jnp.float32)
        + grad_pair_two
    )
    feed_shares = (
        expand_weight_grad,
        expand_bias_grad,
        reduce_weight_grad,
        reduce_bias_grad,
        second_gain_grad,
        second_shift_grad,
    )
    grad_pair_one, first_gain_grad, first_shift_grad = norm_backward(
        grad_first, first_normed, first_inverse, first_gain[0]
    )
    grad_branch16 = grad_pair_one.astype(jnp.bfloat16)
    merge_weight_grad = jnp.einsum(
        "td,te->de", attended16, grad_branch16, preferred_element_type=jnp.float32
    )
    merge_bias_grad = jnp.sum(grad_branch16.astype(jnp.float32), axis=0)
    grad_attended16 = jnp.einsum(
        "te,de->td", grad_branch16, merge_weight[0], preferred_element_type=jnp.float32
    ).astype(jnp.bfloat16)
    grad_attended_blocks = grad_attended16.reshape(block_count, BLOCK, HEADS, HEAD)

    def attend_backward(members):
        query_block, key_block, value_block, grad_out, log_total = members
        scores = masked_scores(query_block, key_block, same_sequence)
        probs = jnp.exp(scores - log_total[..., None])
        probs16 = probs.astype(jnp.bfloat16)
        grad_value = jnp.einsum(
            "hqk,qhd->khd", probs16, grad_out, preferred_element_type=jnp.float32
        )
        grad_probs = jnp.einsum(
            "qhd,khd->hqk", grad_out, value_block, preferred_element_type=jnp.float32
        )
        grad_scores16 = (
            probs * (grad_probs - jnp.sum(probs * grad_probs, axis=-1, keepdims=True))
        ).astype(jnp.bfloat16)
        grad_query = jnp.einsum(
            "hqk,khd->qhd", grad_scores16, key_block, preferred_element_type=jnp.float32
        ) * (1.0 / math.sqrt(HEAD))
        grad_key = jnp.einsum(
            "hqk,qhd->khd", grad_scores16, query_block, preferred_element_type=jnp.float32
        ) * (1.0 / math.sqrt(HEAD))
        return (grad_query, grad_key, grad_value)

    grad_queries, grad_keys, grad_values = lax.map(
        attend_backward, (queries, keys_all, values_all, grad_attended_blocks, log_totals)
    )
    grad_packed16 = (
        jnp.stack([grad_queries, grad_keys, grad_values], axis=2)
        .reshape(row_count, 3 * model_width)
        .astype(jnp.bfloat16)
    )
    attend_weight_grad = jnp.einsum(
        "td,te->de", token_rows, grad_packed16, preferred_element_type=jnp.float32
    )
    packed_sums = jnp.sum(grad_packed16.astype(jnp.float32), axis=0)
    attend_bias_grad = jnp.concatenate([packed_sums[:model_width], packed_sums[2 * model_width :]])
    grad_rows = (
        jnp.einsum("te,de->td", grad_packed16, attend_weight[0], preferred_element_type=jnp.float32)
        + grad_pair_one
    )
    every_share = (
        lax.psum_scatter(attend_weight_grad, "dp", scatter_dimension=0, tiled=True),
        lax.psum_scatter(attend_bias_grad, "dp", scatter_dimension=0, tiled=True),
        lax.psum_scatter(merge_weight_grad, "dp", scatter_dimension=0, tiled=True),
        lax.psum_scatter(merge_bias_grad, "dp", scatter_dimension=0, tiled=True),
        lax.psum_scatter(first_gain_grad, "dp", scatter_dimension=0, tiled=True),
        lax.psum_scatter(first_shift_grad, "dp", scatter_dimension=0, tiled=True),
        lax.psum_scatter(expand_weight_grad, "dp", scatter_dimension=0, tiled=True),
        lax.psum_scatter(expand_bias_grad, "dp", scatter_dimension=0, tiled=True),
        lax.psum_scatter(reduce_weight_grad, "dp", scatter_dimension=0, tiled=True),
        lax.psum_scatter(reduce_bias_grad, "dp", scatter_dimension=0, tiled=True),
        lax.psum_scatter(second_gain_grad, "dp", scatter_dimension=0, tiled=True),
        lax.psum_scatter(second_shift_grad, "dp", scatter_dimension=0, tiled=True),
    )
    attend_shares = every_share[:6]
    feed_shares = every_share[6:]
    return (
        final.astype(jnp.bfloat16)[None],
        loss_value,
        grad_rows.astype(jnp.bfloat16)[None],
        attend_shares[0][None],
        attend_shares[1][None],
        attend_shares[2][None],
        attend_shares[3][None],
        attend_shares[4][None],
        attend_shares[5][None],
        feed_shares[0][None],
        feed_shares[1][None],
        feed_shares[2][None],
        feed_shares[3][None],
        feed_shares[4][None],
        feed_shares[5][None],
    )


def solution(mesh):
    in_specs = (
        P("pair", "dp", None),
        P("pair", None, None),
        P("pair", None),
        P("pair", None, None),
        P("pair", None),
        P("pair", None),
        P("pair", None),
        P("pair", None, None),
        P("pair", None),
        P("pair", None, None),
        P("pair", None),
        P("pair", None),
        P("pair", None),
        P("pair", "dp", None),
        P(),
        P(),
    )
    out_specs = (
        P("pair", "dp", None),
        P(),
        P("pair", "dp", None),
        P("pair", "dp", None),
        P("pair", "dp"),
        P("pair", "dp", None),
        P("pair", "dp"),
        P("pair", "dp"),
        P("pair", "dp"),
        P("pair", "dp", None),
        P("pair", "dp"),
        P("pair", "dp", None),
        P("pair", "dp"),
        P("pair", "dp"),
        P("pair", "dp"),
    )
    return jax.shard_map(shards, mesh=mesh, in_specs=in_specs, out_specs=out_specs, check_vma=False)
```

profile of v0, /device:TPU:0, one launch (start us, length us, event | category | flops | bytes accessed | tf_op | source)
XLA Modules:
  0.0 755.6 jit_solution(12318492284023606377)
XLA Ops:
  11.0 7.4 add_convert_fusion.1
  18.4 6.6 copy.118
  25.1 8.9 %reshape.260 = bf16[2,512,3,12,64]{1,0,4,3,2:T(2,128)(2,1)} reshape(bf16[1024,2304]{0,1:T(8,128)(2,1)} %copy.118) | data formatting | bytes 9437184 | tf_op jit(solution)/shard_map/reshape | solution.py:80
  45.0 26.2 %while.30 = (s32[]{:T(128)}, bf16[2,512,12,64]{1,3,2,0:T(8,128)(2,1)}, f32[2,12,512]{2,1,0:T(8,128)}, bf16[2,512,12,64]{1,3,2,0:T(8,128)(2,1)}, bf16[2,512,12,64...) while((s32[]{:T(128)}, ...), condition=%wide.region_3.4_spmd.clone, body=%wide.region_0.3_spmd.clone.sunk | while | flops 840165376 | bytes 43987568 | solution.py:95
  84.1 37.8 %multiply_convert_fusion.1 = (bf16[1024,3072]{1,0:T(8,128)(2,1)S(1)}, f32[1024,3072]{1,0:T(8,128)}, f32[1024,3072]{1,0:T(8,128)}) fusion(f32[3072]{0:T(1024)} %bitcast.269, bf16[1,768,3072]{2,1,0:T(8,128)(2,1)} %param.31, f32[1024,768]{1,0:T(8,128)} %copy-done.6, f32[768]{0:T(1024)S(1)} %reduce.9, f32[768]{0:T(1024)S(1)} %reduce.8, ...), kind=kOutput, calls=%fused_computation.62 | convolution fusion | flops 5043388416 | bytes 39348224 | tf_op jit(solution)/shard_map/dot_general | solution.py:106
  121.9 10.0 %fusion.103 = (f32[1024]{0:T(1024)S(1)}, f32[1024,768]{1,0:T(8,128)S(1)}) fusion(f32[768]{0:T(1024)S(1)} %copy-done.46, bf16[1024,3072]{1,0:T(8,128)(2,1)S(1)} %get-tuple-element.395, bf16[1,3072,768]{2,1,0:T(8,128)(2,1)} %param.33, f32[768]{0:T(1024)S(1)} %reduce.9, f32[768]{0:T(1024)S(1)} %reduce.8, f32[1024]{0:T(1024)S(1)} %add_rsqrt_fusion.1, ...), kind=kOutput, calls=%fused_computation.189 | convolution fusion | flops 4837342208 | bytes 17323008 | tf_op jit(solution)/shard_map/dot_general | solution.py:110
  139.2 45.5 %all-gather = bf16[512,1,768]{2,0,1:T(8,128)(2,1)S(1)} all-gather(bf16[16,1,768]{2,0,1:T(8,128)(2,1)S(1)} %copy.142), channel_id=2, replica_groups=mesh['pair'=2,'dp'=16] {'pair','dp'}, dimensions={0}, use_global_device_ids=true | all-gather | bytes 811008 | tf_op jit(solution)/shard_map/all_gather | solution.py:118
  195.2 8.6 %gather_fusion = f32[1024]{0:T(1024)S(1)} fusion(f32[256,64]{0,1:T(8,128)} %get-tuple-element.420, s32[1024]{0:T(1024)S(1)} %reshape.270), kind=kCustom, calls=%fused_computation | custom fusion | bytes 16384 | tf_op jit(solution)/shard_map/jit(take_along_axis)/gather | solution.py:129
  222.8 19.3 %convert_reduce_fusion = (f32[3072]{0:T(1024)}, bf16[1024,3072]{1,0:T(8,128)(2,1)}) fusion(f32[1024,3072]{1,0:T(8,128)} %get-tuple-element.396, bf16[1,3072,768]{2,1,0:T(8,128)(2,1)} %param.33, f32[1024,768]{1,0:T(8,128)} %get-tuple-element.384, f32[1024,3072]{1,0:T(8,128)} %get-tuple-element.416, f32[3072]{0:T(1024)S(1)} %bitcast.270), kind=kOutput, calls=%fused_computation.60 | convolution fusion | flops 4886098944 | bytes 39346176 | tf_op jit(solution)/shard_map/td,fd->tf/dot_general | solution.py:181
  242.1 11.6 %multiply_reduce_fusion.2 = (f32[768]{0:T(1024)}, f32[1024]{0:T(1024)S(1)}, f32[1024]{0:T(1024)S(1)}, f32[768]{0:T(1024)}, f32[1024,768]{1,0:T(8,128)S(1)}) fusion(f32[1024,768]{1,0:T(8,128)} %copy-done.6, f32[1024]{0:T(1024)S(1)} %add_rsqrt_fusion.1, f32[1024]{0:T(1024)S(1)} %broadcast_multiply_fusion.5, f32[768]{0:T(1024)S(1)} %copy-done.33, ...), kind=kOutput, calls=%fused_computation.94 | convolution fusion | flops 4839698432 | bytes 20472832 | tf_op jit(solution)/shard_map/tf,df->td/dot_general | solution.py:191
  273.1 54.3 %while.31 = (s32[]{:T(128)}, bf16[2,512,12,64]{1,3,2,0:T(8,128)(2,1)}, bf16[2,512,12,64]{1,3,2,0:T(8,128)(2,1)}, bf16[2,512,12,64]{1,3,2,0:T(8,128)(2,1)}, bf16[...) while((s32[]{:T(128)}, ...), condition=%wide.region_19.20_spmd.clone, body=%wide.region_17.19_spmd.clone.sunk | while | flops 2061494272 | bytes 162659760 | solution.py:237
  276.7 6.9 multiply_reduce_fusion.10
  283.6 7.1 multiply_convert_fusion.4
  303.9 6.9 multiply_reduce_fusion.10
  310.8 7.1 multiply_convert_fusion.4
  332.3 9.4 %copy.133 = bf16[2,512,3,12,64]{1,0,4,3,2:T(2,128)(2,1)} copy(bf16[2,512,3,12,64]{1,4,3,0,2:T(8,128)(2,1)} %get-tuple-element.388) | data formatting | bytes 9437184 | tf_op jit(solution)/shard_map/stack | solution.py:241
  353.7 8.0 %copy.139 = f32[768,2304]{1,0:T(8,128)} copy(f32[768,2304]{0,1:T(8,128)} %convolution_bitcast_fusion) | data formatting | bytes 14155776
  367.3 11.2 %fusion.92 = f32[3072,768]{1,0:T(8,128)} fusion(bf16[1024,3072]{1,0:T(8,128)(2,1)} %copy-done.52, f32[1024,768]{1,0:T(8,128)} %get-tuple-element.384), kind=kOutput, calls=%fused_computation.181 | convolution fusion | flops 4832624640 | bytes 18874368 | tf_op jit(solution)/shard_map/tf,td->fd/dot_general | solution.py:177
  379.2 11.3 %fusion.95 = f32[768,3072]{1,0:T(8,128)} fusion(bf16[1024,3072]{1,0:T(8,128)(2,1)} %get-tuple-element.423, f32[1024,768]{1,0:T(8,128)} %copy-done.6, f32[768]{0:T(1024)S(1)} %copy-done.42, f32[768]{0:T(1024)S(1)} %copy-done.34, f32[1024]{0:T(1024)S(1)} %copy-done.28, f32[1024]{0:T(1024)S(1)} %copy-done.26), kind=kOutput, calls=%fused_computation.184 | convolution fusion | flops 4835770368 | bytes 18888704 | tf_op jit(solution)/shard_map/td,tf->df/dot_general | solution.py:186
  399.1 60.6 %all-reduce.10 = (f32[1536]{0:T(1024)}, f32[768]{0:T(1024)}, f32[768]{0:T(1024)}, f32[768]{0:T(1024)}, f32[3072]{0:T(1024)}, /*index=5*/f32[768]{0:T(1024)}, f32[768]{0:T(1024)}, f32[768]{0:T(1024)}) all-reduce(f32[1536]{0:T(1024)} %pad_maximum_fusion.2, ...), channel_id=4, replica_groups=mesh['pair'=2,'dp'=16] {'dp'}, use_global_device_ids=true, to_apply=%region_22.23.clone | all-reduce | flops 9216 | bytes 73728
  474.4 7.4 fusion.73
  486.6 29.6 %reduce-scatter.7.cloned.1.call-done = f32[48,768]{1,0:T(8,128)} async-done(((f32[768,768]{1,0:T(8,128)}), f32[48,768]{1,0:T(8,128)}) %reduce-scatter.7.cloned.1.call-update) | async-done | bytes 147472 | tf_op jit(solution)/shard_map/reduce_scatter | solution.py:257
  516.2 115.1 %reduce-scatter.11.cloned.1.call-done = f32[192,768]{1,0:T(8,128)} async-done(((f32[3072,768]{1,0:T(8,128)}), f32[192,768]{1,0:T(8,128)}) %reduce-scatter.11.cloned.1.call-update) | async-done | bytes 589840 | tf_op jit(solution)/shard_map/reduce_scatter | solution.py:263
  631.3 116.2 %reduce-scatter.9.cloned.1.call-done = f32[48,3072]{1,0:T(8,128)} async-done(((f32[768,3072]{1,0:T(8,128)}), f32[48,3072]{1,0:T(8,128)}) %reduce-scatter.9.cloned.1.call-update) | async-done | bytes 589840 | tf_op jit(solution)/shard_map/reduce_scatter | solution.py:261
  (243 shorter events, 184.0 us)
Async XLA Ops:
  7.2 474.6 %reduce-scatter.13.cloned.1.call-start = ((), (), s32[]{:S(2)}) async-start(), calls=%async_computation.7 | async-start | bytes 7520256
  79.9 173.8 %copy-start.25 = (f32[1024]{0:T(1024)}, f32[1024]{0:T(1024)S(1)}, u32[]{:S(2)}) copy-start(f32[1024]{0:T(1024)S(1)} %broadcast_multiply_fusion.5) | copy-start | bytes 12292
  82.0 171.6 %copy-start.27 = (f32[1024]{0:T(1024)}, f32[1024]{0:T(1024)S(1)}, u32[]{:S(2)}) copy-start(f32[1024]{0:T(1024)S(1)} %add_rsqrt_fusion.1) | copy-start | bytes 12292
  82.0 39.8 %copy-start.32 = (f32[768]{0:T(1024)}, f32[768]{0:T(1024)S(1)}, u32[]{:S(2)}) copy-start(f32[768]{0:T(1024)S(1)} %reduce.8) | copy-start | bytes 9220
  82.8 39.1 %copy-start.41 = (f32[768]{0:T(1024)}, f32[768]{0:T(1024)S(1)}, u32[]{:S(2)}) copy-start(f32[768]{0:T(1024)S(1)} %reduce.9) | copy-start | bytes 9220
  84.1 37.8 %copy-start.7 = (f32[1024,768]{1,0:T(8,128)S(1)}, f32[1024,768]{1,0:T(8,128)}, u32[]{:S(2)}) copy-start(f32[1024,768]{1,0:T(8,128)} %copy-done.6) | copy-start | bytes 9437188
  84.1 37.8 %copy-start.46 = (f32[768]{0:T(1024)S(1)}, f32[768]{0:T(1024)}, u32[]{:S(2)}) copy-start(f32[768]{0:T(1024)} %reduce.10) | copy-start | bytes 9220
  121.8 10.1 %copy-start.52 = (bf16[1024,3072]{1,0:T(8,128)(2,1)}, bf16[1024,3072]{1,0:T(8,128)(2,1)S(1)}, u32[]{:S(2)}) copy-start(bf16[1024,3072]{1,0:T(8,128)(2,1)S(1)} %get-tuple-element.395) | copy-start | bytes 18874372
  132.0 7.2 copy-start.29
  134.1 52.3 %copy-start.35 = (f32[1024]{0:T(1024)}, f32[1024]{0:T(1024)S(1)}, u32[]{:S(2)}) copy-start(f32[1024]{0:T(1024)S(1)} %add_rsqrt_fusion) | copy-start | bytes 12292
  139.1 52.8 %copy-start.44 = (s32[256,4,1]{0,1,2:T(4,128)S(1)}, s32[256,4,1]{0,1,2:T(4,128)}, u32[]{:S(2)}) copy-start(s32[256,4,1]{0,1,2:T(4,128)} %bitcast_or_fusion) | copy-start | bytes 12292
  222.8 19.3 %copy-start.33 = (f32[768]{0:T(1024)S(1)}, f32[768]{0:T(1024)}, u32[]{:S(2)}) copy-start(f32[768]{0:T(1024)} %copy-done.32) | copy-start | bytes 9220
  242.1 11.6 %copy-start.8 = (f32[1024,768]{1,0:T(8,128)S(1)}, f32[1024,768]{1,0:T(8,128)}, u32[]{:S(2)}) copy-start(f32[1024,768]{1,0:T(8,128)} %copy-done.6) | copy-start | bytes 9437188
  283.6 7.1 copy-start.1
  283.6 7.1 copy-start.14
  310.8 7.1 copy-start.14
  361.7 154.5 %reduce-scatter.7.cloned.1.call-start = ((), (), s32[]{:S(2)}) async-start(), calls=%async_computation.4 | async-start | bytes 2506752 | tf_op jit(solution)/shard_map/reduce_scatter | solution.py:257
  367.2 264.0 %reduce-scatter.11.cloned.1.call-start = ((), (), s32[]{:S(2)}) async-start(), calls=%async_computation.6 | async-start | bytes 10027008 | tf_op jit(solution)/shard_map/reduce_scatter | solution.py:263
  378.5 369.0 %reduce-scatter.9.cloned.1.call-start = ((), (), s32[]{:S(2)}) async-start(), calls=%async_computation.5 | async-start | bytes 10027008 | tf_op jit(solution)/shard_map/reduce_scatter | solution.py:261
  390.5 80.2 %copy-start.31 = (f32[1024]{0:T(1024)S(1)}, f32[1024]{0:T(1024)}, u32[]{:S(2)}) copy-start(f32[1024]{0:T(1024)} %copy-done.29) | copy-start | bytes 12292
  390.5 80.2 %copy-start.37 = (f32[1024]{0:T(1024)S(1)}, f32[1024]{0:T(1024)}, u32[]{:S(2)}) copy-start(f32[1024]{0:T(1024)} %copy-done.35) | copy-start | bytes 12292
  390.5 80.2 %copy-start.39 = (f32[768]{0:T(1024)S(1)}, f32[768]{0:T(1024)}, u32[]{:S(2)}) copy-start(f32[768]{0:T(1024)} %reduce.11) | copy-start | bytes 9220
  390.5 80.2 %copy-start.43 = (f32[768]{0:T(1024)S(1)}, f32[768]{0:T(1024)}, u32[]{:S(2)}) copy-start(f32[768]{0:T(1024)} %reduce.12) | copy-start | bytes 9220
  461.7 12.7 %copy-start.19 = (f32[1024,768]{1,0:T(8,128)S(1)}, f32[1024,768]{1,0:T(8,128)}, u32[]{:S(2)}) copy-start(f32[1024,768]{1,0:T(8,128)} %copy-done.18) | copy-start | bytes 9437188
  (44 other events, 114.4 us)
Sparse Core Ops, SparseCore 0:
  361.8 86.8 reduce-scatter.12
  453.5 62.6 reduce-scatter.6
  520.9 110.3 reduce-scatter.10
  636.3 111.0 reduce-scatter.8
where the time goes:
time: 766 us; the launch traced here: 756 us
  waiting for transfers between devices  261 us (34%)
  matrix products  190 us (25%)
  local copies, waits for them, and re-layouts  123 us (16%)
  blocking collectives  106 us (14%)
  other arithmetic  56.7 us (7%)
  between operations  18.5 us (2%)
    reduce_scatter x1, waiting for transfers between devices, shards(): lax.psum_scatter(expand_weight_grad, 'dp', scatter_dimension=0, tiled=True)  116 us
    reduce_scatter x1, waiting for transfers between devices, shards(): lax.psum_scatter(reduce_weight_grad, 'dp', scatter_dimension=0, tiled=True)  115 us
    unnamed x1, blocking collectives  60.6 us
    all_gather x1, blocking collectives, shards(): every_leading = lax.all_gather(leading, ('pair', 'dp'), axis=0, tiled=True)  45.5 us
    unnamed x98, local copies, waits for them, and re-layouts  39.6 us
    dot_general x1, matrix products, shards(): jnp.dot(first16, expand_weight[0], preferred_element_type=jnp.float32)  37.8 us
    reduce_scatter x1, waiting for transfers between devices, shards(): lax.psum_scatter(merge_weight_grad, 'dp', scatter_dimension=0, tiled=True)  29.6 us
    dot_general x1, matrix products, shards(): jnp.einsum('td,fd->tf', grad_second16, reduce_weight[0], preferred_elemen...  19.3 us
  transfers between devices with their start and end apart: 4, of which 3 were waited for; matrix products, arithmetic and copies ran while one was open for 8% of the time, Pallas kernels for 0%

commit v1 on v0

--- a/solution.py
+++ b/solution.py
@@ -4,6 +4,8 @@
 import jax
 import jax.numpy as jnp
 from jax import lax
+from jax.experimental import pallas as pl
+from jax.experimental.pallas import tpu as pltpu
 from jax.sharding import PartitionSpec as P
 
 D = 768
@@ -13,11 +15,842 @@
 PLEN = 256
 BLOCK = 512
 KPOS = 4
-
+SEQ = 256
+PAIRS = HEADS // 2
+WIDE = 2 * HEAD
 
 eps = 1e-06
 loss_weight = 32.0
 negative = -1e30
+VMEM_BYTES = 64 * 1024 * 1024
+TOGETHER = 1
+MESH = pl.DeviceIdType.MESH
+f32 = jnp.float32
+bf16 = jnp.bfloat16
+
+
+def dot_nn(a, b):
+    return lax.dot_general(a, b, (((1,), (0,)), ((), ())), preferred_element_type=f32)
+
+
+def dot_nt(a, b):
+    return lax.dot_general(a, b, (((1,), (1,)), ((), ())), preferred_element_type=f32)
+
+
+def dot_tn(a, b):
+    return lax.dot_general(a, b, (((0,), (0,)), ((), ())), preferred_element_type=f32)
+
+
+def gelu_both(v):
+    density = jnp.exp(v * v * -0.5)
+    t = 1.0 / (1.0 + jnp.abs(v) * (0.3275911 / math.sqrt(2.0)))
+    poly = 0.5 * 1.061405429
+    poly = poly * t + 0.5 * -1.453152027
+    poly = poly * t + 0.5 * 1.421413741
+    poly = poly * t + 0.5 * -0.284496736
+    poly = poly * t + 0.5 * 0.254829592
+    tail = poly * t * density
+    below = jnp.where(v >= 0.0, 1.0 - tail, tail)
+    return v * below, below + v * density * (1.0 / math.sqrt(2.0 * math.pi))
+
+
+def norm_stats(values):
+    centred = values - jnp.mean(values, axis=-1, keepdims=True)
+    inverse = lax.rsqrt(jnp.mean(centred * centred, axis=-1, keepdims=True) + eps)
+    return centred * inverse, inverse
+
+
+def norm_back(upstream, normed, inverse, gain):
+    scaled = upstream * gain
+    return inverse * (
+        scaled
+        - jnp.mean(scaled, axis=-1, keepdims=True)
+        - normed * jnp.mean(scaled * normed, axis=-1, keepdims=True)
+    )
+
+
+def scoped(f):
+    def inner(*args):
+        with jax.named_scope(f.__name__):
+            return f(*args)
+
+    return inner
+
+
+def colsum(values):
+    return jnp.sum(values, axis=0, keepdims=True)
+
+
+SMALL = ("ab", "mb", "g1", "h1", "eb", "rb", "g2", "h2", "post", "cnt")
+INPUTS = ("tok_hbm", "wa_hbm", "wm_hbm", "we_hbm", "wr_hbm", "cot_hbm") + tuple(k + "_hbm" for k in SMALL)
+OUTPUTS = ("act_hbm", "loss", "dx_hbm", "dwa_hbm", "dwm_hbm", "dwe_hbm", "dwr_hbm", "dab", "dmb", "dg1", "dh1", "deb", "drb", "dg2", "dh2")
+
+
+def layer_kernel(n, rows, ff, names, *refs):
+    r = dict(zip(names, refs, strict=True))
+    wm, we, wr, tok, pk, att_t = (r[k] for k in ("wm", "we", "wr", "tok", "pk", "att_t"))
+    low1, n1, fb, hid, gp, cot = (r[k] for k in ("low1", "n1", "fb", "hid", "gp", "cot"))
+    lse, s1, s2, mask, red = (r[k] for k in ("lse", "s1", "s2", "mask", "red"))
+    stage32, cls, vec, vec_out = (r[k] for k in ("stage32", "cls", "vec", "vec_out"))
+    ab, mb, g1, h1, eb, rb, g2, h2 = (r[k] for k in ("ab", "mb", "g1", "h1", "eb", "rb", "g2", "h2"))
+    nz = n // 4
+    part = D // n
+    half = D // 2
+    blocks = rows // SEQ
+    ffc = ff // D
+    thirds = D // SEQ
+    shard = ff // n
+    extra = rows // QLEN
+    y = lax.axis_index("pair")
+    me = lax.axis_index("dp")
+    z = me // 4
+    x = (me // 2) % 2
+    c = me % 2
+
+    sibling = {"dp": z * 4 + x * 2 + (1 - c)}
+    across = {"dp": z * 4 + (1 - x) * 2 + c}
+    other_pair = {"pair": 1 - y}
+    along = [{"dp": ((z + k) % nz) * 4 + x * 2 + c} for k in range(1, nz)]
+    partners = [sibling, across, other_pair] + along
+    barrier = pltpu.get_barrier_semaphore()
+    for partner in partners:
+        pl.semaphore_signal(barrier, inc=1, device_id=partner, device_id_type=MESH)
+
+    def remote(source, target, send, recv, device):
+        return pltpu.make_async_remote_copy(
+            src_ref=source,
+            dst_ref=target,
+            send_sem=send,
+            recv_sem=recv,
+            device_id=device,
+            device_id_type=MESH,
+        )
+
+    loads = {}
+
+    def load(key, source, target):
+        loads[key] = pltpu.make_async_copy(source, target, r["load_sem"].at[len(loads)])
+        loads[key].start()
+
+    load("tok", r["tok_hbm"], tok)
+    for j in range(3):
+        for k in range(thirds):
+            load(
+                ("wa", j, k),
+                r["wa_hbm"].at[:, pl.ds(j * D + k * SEQ, SEQ)],
+                red.at[j, pl.ds(k * D, D), :],
+            )
+    for key in SMALL:
+        load(key, r[key + "_hbm"], r[key])
+    load("wm", r["wm_hbm"], wm)
+    load("we", r["we_hbm"], we)
+    load("wr", r["wr_hbm"], wr)
+    load("cot", r["cot_hbm"], cot)
+
+    row_id = lax.broadcasted_iota(jnp.int32, (SEQ, SEQ), 0)
+    col_id = lax.broadcasted_iota(jnp.int32, (SEQ, SEQ), 1)
+    together = ((row_id // QLEN) == (col_id // QLEN)) | (row_id * 0 + y == 1)
+    mask[...] = jnp.where(together, 0.0, negative)
+    vec[...] = jnp.zeros_like(vec)
+    first_head = lax.broadcasted_iota(jnp.int32, (SEQ, WIDE), 1) < HEAD
+
+    def split_heads(pair):
+        zero = jnp.zeros_like(pair)
+        return jnp.where(first_head, pair, zero), jnp.where(first_head, zero, pair)
+
+    def block_rows(b, shift=0):
+        return pl.ds(pl.multiple_of(b * SEQ + shift, 16), SEQ)
+
+    def block_lanes(b):
+        return pl.ds(pl.multiple_of(b * SEQ, SEQ), SEQ)
+
+    def wide(h):
+        return pl.ds(pl.multiple_of(h * WIDE, WIDE), WIDE)
+
+    def loop(first, last, body):
+        def step(i, carry):
+            with jax.named_scope(body.__name__):
+                body(i)
+            return carry
+
+        lax.fori_loop(first, last, step, 0)
+
+    loads["tok"].wait()
+    for key in SMALL:
+        loads[key].wait()
+    for j in range(3):
+        for k in range(thirds):
+            loads[("wa", j, k)].wait()
+
+    def project(b):
+        at = block_rows(b)
+        here = tok[at, :]
+        for j in range(3):
+            for k in range(thirds):
+                lanes = slice(k * SEQ, (k + 1) * SEQ)
+                out = dot_nn(here, red[j, k * D : (k + 1) * D, :])
+                if j == 0:
+                    out = (out + ab[:, lanes]) * (1.0 / math.sqrt(HEAD))
+                elif j == 2:
+                    out = out + ab[:, D + k * SEQ : D + (k + 1) * SEQ]
+                pk[j, at, lanes] = out.astype(bf16)
+
+    loop(0, blocks, project)
+
+    def attend_pair(b, h):
+        at = block_rows(b)
+        lanes = wide(h)
+        key_pair = pk[1, at, lanes]
+        value_t = pk[2, at, lanes].T
+        mixed = []
+        for s, query in enumerate(split_heads(pk[0, at, lanes])):
+            scores = dot_nt(key_pair, query) + mask[...]
+            peak = jnp.max(scores, axis=0, keepdims=True)
+            weight = jnp.exp(scores - peak)
+            total = jnp.sum(weight, axis=0, keepdims=True)
+            lse[2 * (b * PAIRS + h) + s] = peak + jnp.log(total)
+            out = dot_nn(value_t[s * HEAD : (s + 1) * HEAD], weight.astype(bf16))
+            mixed.append(out * (1.0 / total))
+        att_t[wide(h), block_lanes(b)] = jnp.concatenate(mixed, axis=0).astype(bf16)
+
+    def attend(i):
+        per = PAIRS // TOGETHER
+        for k in range(TOGETHER):
+            attend_pair(i // per, (i % per) * TOGETHER + k)
+
+    loop(0, blocks * (PAIRS // TOGETHER), attend)
+
+    loads["wm"].wait()
+
+    def merge(b):
+        at = block_rows(b)
+        branch = dot_tn(att_t[:, block_lanes(b)], wm[...]) + mb[...]
+        normed, inverse = norm_stats(tok[at, :].astype(f32) + branch)
+        first = normed * g1[...] + h1[...]
+        n1[at, :] = normed.astype(bf16)
+        s1[at, :] = inverse
+        fb[at, :] = first
+        low1[at, :] = first.astype(bf16)
+
+    loop(0, blocks, merge)
+
+    loads["we"].wait()
+    loads["wr"].wait()
+
+    def act_stage(b, k):
+        return red.at[k, block_rows(b), :]
+
+    def act_copies(b):
+        return [
+            pltpu.make_async_copy(
+                act_stage(b, k),
+                r["act_hbm"].at[block_rows(b), pl.ds(k * SEQ, SEQ)],
+                r["act_sem"].at[b, k],
+            )
+            for k in range(thirds)
+        ]
+
+    def feed_chunk(here, j):
+        inner = dot_nn(here, we[:, j * D : (j + 1) * D]) + eb[:, j * D : (j + 1) * D]
+        hidden, slope = gelu_both(inner)
+        hidden = hidden.astype(bf16)
+        return hidden, slope, dot_nn(hidden, wr[j * D : (j + 1) * D, :])
+
+    def feed(b, halfway=None):
+        at = block_rows(b)
+        here = low1[at, :]
+        total = rb[...]
+        for j in range(ffc):
+            if j == ffc // 2 and halfway is not None:
+                halfway()
+            hidden, slope, out = feed_chunk(here, j)
+            hid[j, :, block_lanes(b)] = hidden.T
+            gp[j, at, :] = slope.astype(bf16)
+            total = total + out
+        normed, inverse = norm_stats(fb[at, :] + total)
+        final = (normed * g2[...] + h2[...]).astype(bf16)
+        fb[at, :] = normed
+        s2[at, :] = inverse
+        for k in range(thirds):
+            act_stage(b, k)[...] = final[:, k * SEQ : (k + 1) * SEQ]
+        for copy in act_copies(b):
+            copy.start()
+
+    for k in range(extra):
+        stage32[k : k + 1, :] = fb[k * QLEN : k * QLEN + 1, :]
+    slot = ((c * 2 + y) * 2 + x) * nz + z
+    first_rows = stage32[0:extra, :]
+    first_low = first_rows.astype(bf16)
+    leading = rb[...]
+    for j in range(ffc):
+        leading = leading + feed_chunk(first_low, j)[2]
+    leading = norm_stats(first_rows + leading)[0] * g2[...] + h2[...]
+    cls[pl.ds(pl.multiple_of(slot * extra, extra), extra), :] = leading.astype(bf16)
+
+    def gather(stage, first, count, device):
+        part_of = cls.at[pl.ds(pl.multiple_of(first * extra, extra), count * extra), :]
+        return remote(part_of, part_of, r["ag_send"].at[stage], r["ag_recv"].at[stage], device)
+
+    pl.semaphore_wait(barrier, len(partners))
+    gather_z = [gather(k, slot, 1, along[k]) for k in range(nz - 1)]
+    gather_x = gather(nz - 1, ((c * 2 + y) * 2 + x) * nz, nz, across)
+    gather_y = gather(nz, (c * 2 + y) * 2 * nz, 2 * nz, other_pair)
+    gather_c = [gather(nz + 1 + e, (c * 2 + [y, 1 - y][e]) * 2 * nz, 2 * nz, sibling) for e in range(2)]
+    for copy in gather_z:
+        copy.start()
+
+    def feed_next(b):
+        feed(b)
+
+        @pl.when(b == 0)
+        def _():
+            for copy in gather_z:
+                copy.wait()
+            gather_x.start()
+
+        @pl.when(b == 1)
+        def _():
+            gather_x.wait()
+            gather_y.start()
+            gather_c[0].start()
+
+    def last_gather():
+        gather_y.wait()
+        gather_c[1].start()
+
+    loop(0, blocks - 1, feed_next)
+    feed(blocks - 1, last_gather)
+    gather_c[0].wait()
+    gather_c[1].wait()
+
+    nq = n * extra
+    spare = blocks * SEQ
+    for d in range(n):
+        there = ((d % 2) * 4 + (d // 2) % 2) * nz + d // 4
+        for e in range(2):
+            block = there + e * 2 * nz
+            for k in range(thirds):
+                red[k, spare + e * nq + d * extra : spare + e * nq + (d + 1) * extra, :] = cls[
+                    block * extra : (block + 1) * extra, k * SEQ : (k + 1) * SEQ
+                ]
+
+    def gathered(e):
+        return jnp.concatenate([red[k, spare + e * nq : spare + (e + 1) * nq, :] for k in range(thirds)], axis=1)
+
+    question = gathered(0)
+    passage = gathered(1)
+    root_width = math.sqrt(D)
+    match = dot_nt(passage, question) * (1.0 / root_width)
+    place = lax.broadcasted_iota(jnp.int32, (nq, nq), 0)
+    number = place // (PLEN // QLEN)
+    real = place % (PLEN // QLEN) == 0
+    listed = jnp.zeros((nq, nq), jnp.int32)
+    for k in range(KPOS):
+        wanted = jnp.where(r["cnt"][...] > k, r["post"][k : k + 1, :], -1)
+        listed = jnp.where(number == wanted, 1, listed)
+    listed = (listed == 1) & real
+    all_scores = jnp.where(real, match, negative)
+    all_peak = jnp.max(all_scores, axis=0, keepdims=True)
+    all_total = jnp.sum(jnp.exp(all_scores - all_peak), axis=0, keepdims=True)
+    lse_all = all_peak + jnp.log(all_total)
+    live_scores = jnp.where(listed, match, negative)
+    live_peak = jnp.max(live_scores, axis=0, keepdims=True)
+    live_total = jnp.sum(jnp.where(listed, jnp.exp(live_scores - live_peak), 0.0), axis=0, keepdims=True)
+    lse_live = live_peak + jnp.log(live_total)
+    r["loss"][...] = jnp.sum(lse_all - lse_live, axis=1, keepdims=True) * (1.0 / nq)
+    grad_match = jnp.exp(all_scores - lse_all) - jnp.where(listed, jnp.exp(live_scores - lse_live), 0.0)
+    grad_match = (loss_weight * grad_match).astype(bf16)
+
+    @pl.when(y == 0)
+    def _():
+        stage32[0:nq, :] = dot_tn(grad_match, gathered(1)) * (1.0 / root_width)
+
+    @pl.when(y == 1)
+    def _():
+        stage32[0:nq, :] = dot_nn(grad_match, gathered(0)) * (1.0 / root_width)
+
+    loads["cot"].wait()
+
+    per_block = SEQ // QLEN
+    own_rows = pl.ds(pl.multiple_of(me * extra, extra), extra)
+    stage32[nq : nq + extra, :] = stage32[own_rows, :]
+    top_row = lax.broadcasted_iota(jnp.int32, (8, D), 0) == 0
+
+    def second_back(b):
+        at = block_rows(b)
+        given = cot[at, :].astype(f32)
+        pieces = []
+        for k in range(per_block):
+            own = stage32[pl.ds(nq + b * per_block + k, 1), :]
+            pieces.append(given[k * QLEN : k * QLEN + 8] + jnp.where(top_row, own, 0.0))
+            pieces.append(given[k * QLEN + 8 : (k + 1) * QLEN])
+        upstream = jnp.concatenate(pieces, axis=0)
+        normed = fb[at, :]
+        grad = norm_back(upstream, normed, s2[at, :], g2[...])
+        low = grad.astype(bf16)
+        fb[at, :] = grad
+        cot[at, :] = low
+        vec[5 + ffc : 6 + ffc, :] += colsum(low.astype(f32))
+        vec[6 + ffc : 7 + ffc, :] += colsum(upstream * normed)
+        vec[7 + ffc : 8 + ffc, :] += colsum(upstream)
+
+    loop(0, blocks, second_back)
+
+    units = (
+        [(red, k, shard, "r", k) for k in range(thirds)]
+        + [(hid, j, part, "w", j) for j in range(ffc)]
+        + [(gp, j, part, "w", ffc + j) for j in range(4)]
+    )
+    unit_out = (
+        [r["dwr_hbm"].at[:, pl.ds(k * SEQ, SEQ)] for k in range(thirds)]
+        + [r["dwe_hbm"].at[:, pl.ds(j * D, D)] for j in range(ffc)]
+        + [r["dwm_hbm"]]
+        + [r["dwa_hbm"].at[:, pl.ds(j * D, D)] for j in range(3)]
+    )
+
+    def unit_rows(u, first, count):
+        ref, j, each, kind, _ = units[u]
+        at = pl.ds(pl.multiple_of(first * each, each), count * each)
+        return ref.at[j, at, :] if kind == "r" else ref.at[j, at, pl.ds(0, D)]
+
+    def arrived(u, stage):
+        return r["recv_" + stage + units[u][3]].at[units[u][4]]
+
+    def add_rows(u, first, source, source_first, count):
+        each = units[u][2]
+
+        def step(i):
+            here = unit_rows(u, first + i, 1)
+            more = source[pl.ds(pl.multiple_of((source_first + i) * each, each), each), :]
+            here[...] = (here[...].astype(f32) + more.astype(f32)).astype(bf16)
+
+        loop(0, count, step)
+
+    def core_copy(u):
+        return remote(
+            unit_rows(u, (1 - c) * (n // 2), n // 2),
+            arrived(u, "c"),
+            r["c_send"].at[u],
+            r["c_recv"].at[u],
+            sibling,
+        )
+
+    def across_copy(u):
+        return remote(
+            unit_rows(u, c * (n // 2) + (1 - x) * nz, nz),
+            arrived(u, "x"),
+            r["x_send"].at[u],
+            r["x_recv"].at[u],
+            across,
+        )
+
+    def along_copy(u, k):
+        return remote(
+            unit_rows(u, c * (n // 2) + x * nz + (z + k) % nz, 1),
+            arrived(u, "z").at[k - 1],
+            r["z_send"].at[u, k - 1],
+            r["z_recv"].at[u, k - 1],
+            along[k - 1],
+        )
+
+    def out_stage(u):
+        _, _, each, kind, at = units[u]
+        return r["stage_r" if kind == "r" else "stage32"].at[pl.ds(at * each, each), :]
+
+    def out_copy(u):
+        return pltpu.make_async_copy(out_stage(u), unit_out[u], r["out_sem"].at[u])
+
+    @scoped
+    def core_start(u):
+        core_copy(u).start()
+
+    @scoped
+    def across_start(u):
+        core_copy(u).wait_recv()
+        add_rows(u, c * (n // 2) + (1 - x) * nz, arrived(u, "c"), (1 - x) * nz, nz)
+        across_copy(u).start()
+        add_rows(u, c * (n // 2) + x * nz, arrived(u, "c"), x * nz, nz)
+
+    @scoped
+    def along_start(u):
+        across_copy(u).wait_recv()
+        add_rows(u, c * (n // 2) + x * nz, arrived(u, "x"), 0, nz)
+        for k in range(1, nz):
+            along_copy(u, k).start()
+
+    @scoped
+    def finish(u):
+        total = unit_rows(u, c * (n // 2) + x * nz + z, 1)[...].astype(f32)
+        for k in range(1, nz):
+            along_copy(u, k).wait_recv()
+            total = total + arrived(u, "z")[k - 1].astype(f32)
+        out_stage(u)[...] = total
+        out_copy(u).start()
+
+    def spot(d):
+        return ((d % 2) * 2 + (d // 2) % 2) * nz + d // 4
+
+    def spread(u, result, first):
+        for d in range(first, first + result.shape[0] // part):
+            piece = result[(d - first) * part : (d - first + 1) * part]
+            unit_rows(u, spot(d), 1)[...] = piece.astype(bf16)
+
+    for b in range(blocks):
+        for copy in act_copies(b):
+            copy.wait()
+    for u in range(thirds):
+
+        def reduce_grad(t, u=u):
+            tiles = D // (2 * shard)
+            left = hid[t // tiles, pl.ds(pl.multiple_of((t % tiles) * 2 * shard, 16), 2 * shard), :]
+            result = dot_nn(left, cot[:, u * SEQ : (u + 1) * SEQ]).astype(bf16)
+            for cc in range(2):
+                unit_rows(u, (cc * 2 + t % 2) * nz + t // 2, 1)[...] = result[cc * shard : (cc + 1) * shard]
+
+        loop(0, n // 2, reduce_grad)
+        core_start(u)
+        if u > 0:
+            across_start(u - 1)
+    expand_at = thirds
+    merge_at = thirds + ffc
+    attend_at = merge_at + 1
+
+    for j in range(ffc):
+
+        def inner_back(b, j=j):
+            at = block_rows(b)
+            grad_hidden = dot_nt(cot[at, :], wr[j * D : (j + 1) * D, :])
+            low = (grad_hidden * gp[j, at, :].astype(f32)).astype(bf16)
+            gp[j, at, :] = low
+            vec[5 + j : 6 + j, :] += colsum(low.astype(f32))
+            fb[at, :] += dot_nt(low, we[:, j * D : (j + 1) * D])
+
+        loop(0, blocks, inner_back)
+        if j == 1:
+            along_start(0)
+            across_start(2)
+        elif j == 2:
+            along_start(1)
+            across_start(expand_at)
+        for t in range(2):
+            left = low1[:, t * half : (t + 1) * half]
+            spread(expand_at + j, dot_tn(left, gp[j]), (n // 2) * t)
+        core_start(expand_at + j)
+        if j == 2:
+            finish(0)
+        elif j == 3:
+            along_start(2)
+            across_start(expand_at + 1)
+    load("wa_again", r["wa_hbm"], we.at[:, pl.ds(0, 3 * D)])
+
+    def first_back(b):
+        at = block_rows(b)
+        upstream = fb[at, :]
+        normed = n1[at, :].astype(f32)
+        grad = norm_back(upstream, normed, s1[at, :], g1[...])
+        low = grad.astype(bf16)
+        fb[at, :] = grad
+        cot[at, :] = low
+        vec[2:3, :] += colsum(low.astype(f32))
+        vec[3:4, :] += colsum(upstream * normed)
+        vec[4:5, :] += colsum(upstream)
+        n1[at, :] = dot_nt(low, wm[...]).astype(bf16)
+
+    loop(0, blocks, first_back)
+    for t in range(2):
+        spread(merge_at, dot_nn(att_t[t * half : (t + 1) * half, :], cot[...]), (n // 2) * t)
+    core_start(merge_at)
+    along_start(expand_at)
+    across_start(expand_at + 2)
+    finish(1)
+
+    def attend_back(i):
+        b = i // PAIRS
+        h = i % PAIRS
+        at = block_rows(b)
+        lanes = wide(h)
+        key_pair = pk[1, at, lanes]
+        value_pair = pk[2, at, lanes]
+        key_t = key_pair.T
+        queries = split_heads(pk[0, at, lanes])
+        grads = split_heads(n1[at, lanes])
+        probs = []
+        slopes = []
+        query_grads = []
+        for s in range(2):
+            prob = jnp.exp(dot_nt(key_pair, queries[s]) + mask[...] - lse[2 * i + s])
+            grad_prob = dot_nt(value_pair, grads[s])
+            mean = jnp.sum(prob * grad_prob, axis=0, keepdims=True)
+            slope = (prob * (grad_prob - mean)).astype(bf16)
+            probs.append(prob.astype(bf16))
+            slopes.append(slope)
+            query_grads.append(dot_nn(key_t[s * HEAD : (s + 1) * HEAD], slope))
+        grad_value = dot_nn(jnp.concatenate(probs, axis=1), jnp.concatenate(grads, axis=0)).astype(bf16)
+        grad_key = dot_nn(jnp.concatenate(slopes, axis=1), jnp.concatenate(queries, axis=0)).astype(bf16)
+        grad_query = (jnp.concatenate(query_grads, axis=0) * (1.0 / math.sqrt(HEAD))).T.astype(bf16)
+        pk[0, at, lanes] = grad_query
+        pk[1, at, lanes] = grad_key
+        pk[2, at, lanes] = grad_value
+        vec[0:1, lanes] += colsum(grad_query.astype(f32))
+        vec[1:2, lanes] += colsum(grad_value.astype(f32))
+
+        @pl.when(i == 7)
+        def _():
+            along_start(expand_at + 1)
+            across_start(expand_at + 3)
+            finish(2)
+
+        @pl.when(i == 14)
+        def _():
+            along_start(expand_at + 2)
+            across_start(merge_at)
+            finish(expand_at)
+
+        @pl.when(i == 21)
+        def _():
+            along_start(expand_at + 3)
+            finish(expand_at + 1)
+
+    loop(0, blocks * PAIRS, attend_back)
+
+    for d in range(n):
+        def chunk(row, first, d=d):
+            at = first * part
+            return vec[row + at // D : row + at // D + 1, at % D : at % D + part]
+
+        at = spot(d)
+        for e in range(2):
+            vec_out[at, e : e + 1, 0:part] = chunk(0, 2 * d + e)
+        for e in range(3):
+            vec_out[at, 2 + e : 3 + e, 0:part] = chunk(2 + e, d)
+            vec_out[at, 5 + ffc + e : 6 + ffc + e, 0:part] = chunk(5 + ffc + e, d)
+        for e in range(ffc):
+            vec_out[at, 5 + e : 6 + e, 0:part] = chunk(5, ffc * d + e)
+
+    def vec_part(first, count):
+        return vec_out.at[pl.ds(first, count)]
+
+    mine = c * (n // 2) + x * nz
+    vec_c = remote(
+        vec_part((1 - c) * (n // 2), n // 2), r["vec_c"], r["v_send"].at[0], r["v_recv"].at[0], sibling
+    )
+    vec_x = remote(
+        vec_part(c * (n // 2) + (1 - x) * nz, nz), r["vec_x"], r["v_send"].at[1], r["v_recv"].at[1], across
+    )
+    vec_z = [
+        remote(
+            vec_part(mine + (z + k) % nz, 1),
+            r["vec_z"].at[pl.ds(k - 1, 1)],
+            r["v_send"].at[1 + k],
+            r["v_recv"].at[1 + k],
+            along[k - 1],
+        )
+        for k in range(1, nz)
+    ]
+    vec_c.start()
+
+    for j in range(3):
+        unit = attend_at + j
+        for t in range(2):
+            spread(unit, dot_tn(tok[:, t * half : (t + 1) * half], pk[j]), (n // 2) * t)
+        core_start(unit)
+        if j == 0:
+            vec_c.wait()
+            vec_out[pl.ds(c * (n // 2), n // 2)] += r["vec_c"][...]
+            vec_x.start()
+        elif j == 1:
+            across_start(attend_at)
+            along_start(merge_at)
+            finish(expand_at + 2)
+            vec_x.wait()
+            vec_out[pl.ds(mine, nz)] += r["vec_x"][...]
+            for copy in vec_z:
+                copy.start()
+
+    loads["wa_again"].wait()
+
+    def dx_copy(b):
+        return pltpu.make_async_copy(tok.at[block_rows(b), :], r["dx_hbm"].at[block_rows(b), :], r["dx_sem"].at[b])
+
+    def token_grad(b):
+        at = block_rows(b)
+        total = fb[at, :]
+        for j in range(3):
+            total = total + dot_nt(pk[j, at, :], we[:, j * D : (j + 1) * D])
+        tok[at, :] = total.astype(bf16)
+        dx_copy(b).start()
+
+        @pl.when(b == 0)
+        def _():
+            across_start(attend_at + 1)
+            finish(expand_at + 3)
+
+        @pl.when(b == 3)
+        def _():
+            along_start(attend_at)
+            across_start(attend_at + 2)
+            finish(merge_at)
+
+    loop(0, blocks, token_grad)
+    for copy in vec_z:
+        copy.wait()
+    total = vec_out[mine + z]
+    for k in range(1, nz):
+        total = total + r["vec_z"][k - 1]
+    for e in range(2):
+        r["dab"][:, e * part : (e + 1) * part] = total[e : e + 1, 0:part]
+    for e in range(ffc):
+        r["deb"][:, e * part : (e + 1) * part] = total[5 + e : 6 + e, 0:part]
+    for key, row in (("dmb", 2), ("dg1", 3), ("dh1", 4), ("drb", 5 + ffc), ("dg2", 6 + ffc), ("dh2", 7 + ffc)):
+        r[key][...] = total[row : row + 1, 0:part]
+    along_start(attend_at + 1)
+    finish(attend_at)
+    along_start(attend_at + 2)
+    finish(attend_at + 1)
+    finish(attend_at + 2)
+    for u in range(len(units)):
+        core_copy(u).wait_send()
+        across_copy(u).wait_send()
+        for k in range(1, nz):
+            along_copy(u, k).wait_send()
+        out_copy(u).wait()
+    for b in range(blocks):
+        dx_copy(b).wait()
+
+
+def hand_over_kernel(count, *refs):
+    given, wanted, held = (refs[k * count : (k + 1) * count] for k in range(3))
+    sems = refs[-1]
+    arriving = [pltpu.make_async_copy(given[k], held[k], sems.at[0, k]) for k in range(count)]
+    leaving = [pltpu.make_async_copy(held[k], wanted[k], sems.at[1, k]) for k in range(count)]
+    for copy in arriving:
+        copy.start()
+    for k in range(count):
+        arriving[k].wait()
+        leaving[k].start()
+    for copy in leaving:
+        copy.wait()
+
+
+def fused_shards(n, *args):
+    tokens, cotangent = args[0][0], args[13][0]
+    rows = tokens.shape[0]
+    ff = args[7].shape[2]
+    ffc = ff // D
+    nz = n // 4
+    part = D // n
+    shard = ff // n
+    thirds = D // SEQ
+    extra = rows // QLEN
+    blocks = rows // SEQ
+    wide_units = ffc + 4
+    units = thirds + wide_units
+    wa, wm, we, wr = (args[k][0] for k in (1, 3, 7, 9))
+    small = [args[k] for k in (2, 4, 5, 6, 8, 10, 11, 12)] + [args[14].T, args[15][None, :]]
+    dma = pltpu.SemaphoreType.DMA
+    scratch = dict(
+        zip(SMALL, [pltpu.VMEM(value.shape, value.dtype) for value in small], strict=True),
+        wm=pltpu.VMEM((D, D), bf16),
+        we=pltpu.VMEM((D, ff), bf16),
+        wr=pltpu.VMEM((ff, D), bf16),
+        tok=pltpu.VMEM((rows, D), bf16),
+        pk=pltpu.VMEM((3, rows, D), bf16),
+        att_t=pltpu.VMEM((D, rows), bf16),
+        low1=pltpu.VMEM((rows, D), bf16),
+        n1=pltpu.VMEM((rows, D), bf16),
+        fb=pltpu.VMEM((rows, D), f32),
+        hid=pltpu.VMEM((ffc, D, rows), bf16),
+        gp=pltpu.VMEM((ffc, rows, D), bf16),
+        cot=pltpu.VMEM((rows, D), bf16),
+        lse=pltpu.VMEM((blocks * HEADS, 1, SEQ), f32),
+        s1=pltpu.VMEM((rows, 1), f32),
+        s2=pltpu.VMEM((rows, 1), f32),
+        mask=pltpu.VMEM((SEQ, SEQ), f32),
+        red=pltpu.VMEM((thirds, ff, SEQ), bf16),
+        stage_r=pltpu.VMEM((thirds * shard, SEQ), f32),
+        stage32=pltpu.VMEM((wide_units * part, D), f32),
+        cls=pltpu.VMEM((8 * nz * extra, D), bf16),
+        vec=pltpu.VMEM((16, D), f32),
+        vec_out=pltpu.VMEM((n, 16, 128), f32),
+        vec_c=pltpu.VMEM((n // 2, 16, 128), f32),
+        vec_x=pltpu.VMEM((nz, 16, 128), f32),
+        vec_z=pltpu.VMEM((nz - 1, 16, 128), f32),
+        recv_cr=pltpu.VMEM((thirds, ff // 2, SEQ), bf16),
+        recv_xr=pltpu.VMEM((thirds, ff // 4, SEQ), bf16),
+        recv_zr=pltpu.VMEM((thirds, nz - 1, shard, SEQ), bf16),
+        recv_cw=pltpu.VMEM((wide_units, D // 2, D), bf16),
+        recv_xw=pltpu.VMEM((wide_units, D // 4, D), bf16),
+        recv_zw=pltpu.VMEM((wide_units, nz - 1, part, D), bf16),
+        load_sem=dma((32,)),
+        act_sem=dma((blocks, thirds)),
+        dx_sem=dma((blocks,)),
+        out_sem=dma((units,)),
+        c_send=dma((units,)),
+        c_recv=dma((units,)),
+        x_send=dma((units,)),
+        x_recv=dma((units,)),
+        z_send=dma((units, nz - 1)),
+        z_recv=dma((units, nz - 1)),
+        ag_send=dma((nz + 3,)),
+        ag_recv=dma((nz + 3,)),
+        v_send=dma((nz + 1,)),
+        v_recv=dma((nz + 1,)),
+    )
+    names = list(INPUTS) + list(OUTPUTS) + list(scratch)
+    hbm = pl.BlockSpec(memory_space=pl.ANY)
+    near = pl.BlockSpec(memory_space=pltpu.VMEM)
+    shape = jax.ShapeDtypeStruct
+    shapes = [
+        shape((rows, D), bf16),
+        shape((1, 1), f32),
+        shape((rows, D), bf16),
+        shape((part, 3 * D), f32),
+        shape((part, D), f32),
+        shape((part, ff), f32),
+        shape((ff // n, D), f32),
+        shape((1, 2 * part), f32),
+        shape((1, part), f32),
+        shape((1, part), f32),
+        shape((1, part), f32),
+        shape((1, ff // n), f32),
+        shape((1, part), f32),
+        shape((1, part), f32),
+        shape((1, part), f32),
+    ]
+    outs = pl.pallas_call(
+        partial(layer_kernel, n, rows, ff, names),
+        out_shape=shapes,
+        in_specs=[hbm] * (6 + len(small)),
+        out_specs=[hbm, near] + [hbm] * 5 + [near] * 8,
+        scratch_shapes=list(scratch.values()),
+        compiler_params=pltpu.CompilerParams(
+            collective_id=0, has_side_effects=True, vmem_limit_bytes=VMEM_BYTES
+        ),
+    )(tokens, wa, wm, we, wr, cotangent, *small)
+    act, loss, dx, dwa, dwm, dwe, dwr, dab, dmb, dg1, dh1, deb, drb, dg2, dh2 = pl.pallas_call(
+        partial(hand_over_kernel, len(shapes)),
+        out_shape=shapes,
+        in_specs=[hbm] * len(shapes),
+        out_specs=[hbm] * len(shapes),
+        scratch_shapes=[pltpu.VMEM(out.shape, out.dtype) for out in shapes] + [dma((2, len(shapes)))],
+    )(*outs)
+    return (
+        act[None],
+        loss[0, 0],
+        dx[None],
+        dwa[None],
+        dab,
+        dwm[None],
+        dmb,
+        dg1,
+        dh1,
+        dwe[None],
+        deb,
+        dwr[None],
+        drb,
+        dg2,
+        dh2,
+    )
 
 
 def layer_norm(values, scale_gain, shift_row):
@@ -322,4 +1155,7 @@
         P("pair", "dp"),
         P("pair", "dp"),
     )
-    return jax.shard_map(shards, mesh=mesh, in_specs=in_specs, out_specs=out_specs, check_vma=False)
+    n = mesh.shape["dp"]
+    fits = mesh.shape["pair"] == 2 and n % 4 == 0 and D % n == 0 and (D // n) % 16 == 0
+    body = partial(fused_shards, n) if fits else shards
+    return jax.shard_map(body, mesh=mesh, in_specs=in_specs, out_specs=out_specs, check_vma=False)

time: 766 us -> 161 us (0.21); the launches traced: 756 us -> 161 us
  waiting for transfers between devices: 261 us -> 0 us
  matrix products: 190 us -> 0 us
  Pallas kernels: 0 us -> 160 us
  local copies, waits for them, and re-layouts: 123 us -> 0 us
  blocking collectives: 106 us -> 0 us
  other arithmetic: 56.7 us -> 0 us
  between operations: 18.5 us -> 0.86 us
    reduce_scatter x3 -> x0, waiting for transfers between devices: 261 us -> none  [the longest x1 116 us: shards(): lax.psum_scatter(expand_weight_grad, 'dp', scatter_dimension=0, tiled=True)]
    dot_general x29 -> x0, matrix products: 190 us -> none  [the longest x1 37.8 us: shards(): jnp.dot(first16, expand_weight[0], preferred_element_type=jnp.float32)]
    pallas_call x0 -> x2, Pallas kernels: none -> 160 us  [the longest x1 156 us: fused_shards(): pl.pallas_call(partial(layer_kernel, n, rows, ff, names), out_shape=shape...]
    unnamed x1 -> x0, blocking collectives: 60.6 us -> none
    all_gather x1 -> x0, blocking collectives: 45.5 us -> none  [shards(): every_leading = lax.all_gather(leading, ('pair', 'dp'), axis=0, tiled=True)]
    unnamed x98 -> x0, local copies, waits for them, and re-layouts: 39.6 us -> none
    reduce_sum x11 -> x0, other arithmetic: 24.4 us -> none  [the longest x2 7.05 us: attend_block(): totals = jnp.sum(jnp.exp(scores - peak), axis=-1, keepdims=True)]
    convert_element_type x4 -> x0, other arithmetic: 17.6 us -> none  [the longest x2 14.3 us: attend_backward(): grad_scores16 = (probs * (grad_probs - jnp.sum(probs * grad_probs, axis=-...]
  transfers between devices with their start and end apart: 4 -> 0, of which waited for: 3 -> 0; matrix products, arithmetic and copies ran while one was open for 8% -> 0% of each run, Pallas kernels for 0% -> 0%
where the time goes in v1:
time: 161 us
  Pallas kernels  160 us (99%)
    pallas_call x1, Pallas kernels, fused_shards(): pl.pallas_call(partial(layer_kernel, n, rows, ff, names), out_shape=shape...  156 us
    pallas_call x1, Pallas kernels, fused_shards(): pl.pallas_call(partial(hand_over_kernel, len(shapes)), out_shape=shapes,...  4.58 us

profile of v1, /device:TPU:0, one launch (start us, length us, event | category | flops | bytes accessed | tf_op | source)
XLA Modules:
  0.0 161.3 jit_solution(5090549200860004008)
XLA Ops:
  0.7 155.9 %shard_map.271 = (bf16[1024,768]{1,0:T(8,128)(2,1)}, f32[1,1]{1,0:T(1,128)}, bf16[1024,768]{1,0:T(8,128)(2,1)}, f32[48,2304]{1,0:T(8,128)}, f32[48,768]{1,0:T(8,...) custom-call(bf16[1024,768]{1,0:T(8,128)(2,1)} %bitcast.18, ...), custom_call_target="tpu_custom_call" | custom-call | tf_op jit(solution)/shard_map/pallas_call | solution.py:820
  156.5 4.6 %shard_map.272 = (bf16[1024,768]{1,0:T(8,128)(2,1)}, f32[1,1]{1,0:T(1,128)}, bf16[1024,768]{1,0:T(8,128)(2,1)}, f32[48,2304]{1,0:T(8,128)}, f32[48,768]{1,0:T(8,...) custom-call(bf16[1024,768]{1,0:T(8,128)(2,1)} %get-tuple-element.45., ...), custom_call_target="tpu_custom_call" | custom-call | tf_op jit(solution)/shard_map/pallas_call | solution.py:830

commit v2 on v1

--- a/solution.py
+++ b/solution.py
@@ -1,5 +1,6 @@
 from functools import partial
 import math
+from types import SimpleNamespace
 
 import jax
 import jax.numpy as jnp
@@ -23,7 +24,44 @@
 loss_weight = 32.0
 negative = -1e30
 VMEM_BYTES = 64 * 1024 * 1024
-TOGETHER = 1
+TOGETHER = 6
+BACK_TOGETHER = 2
+LINE = 4
+PIECES = (1, 1, 1, 1, 1, 1, 1, 1, 1, 2, 2)
+MODES = "babbaaaaaaaab"
+SCHEDULE = {
+    "r0": ((0, 0),),
+    "r1": ((0, 1),),
+    "r2_0": ((1, 0),),
+    "r2": ((0, 2), (1, 1),),
+    "i0_0": ((2, 0),),
+    "i0_1": ((1, 2),),
+    "e0": ((0, 3),),
+    "i1_1": ((2, 2), (1, 3),),
+    "e1": ((0, 4),),
+    "i2_0": ((2, 1), (2, 3),),
+    "i2_1": ((3, 0), (1, 4),),
+    "e2": ((0, 5),),
+    "i3_1": ((1, 5), (3, 2), (3, 1),),
+    "e3": ((0, 6),),
+    "f1": ((3, 3),),
+    "f2": ((1, 6),),
+    "f3": ((4, 0),),
+    "m": ((0, 7),),
+    "t1": ((2, 4),),
+    "t2": ((1, 7), (4, 2),),
+    "t5": ((2, 5),),
+    "t6": ((4, 1),),
+    "t10": ((2, 6), (3, 4), (4, 3),),
+    "v": ((0, 13),),
+    "a0": ((0, 8), (3, 5), (1, 13),),
+    "a1": ((0, 9), (0, 10), (2, 7), (1, 8), (2, 13), (4, 4),),
+    "a2": ((0, 11), (0, 12), (3, 6), (1, 9), (1, 10), (4, 5),),
+    "x0": ((1, 11),),
+    "x2": ((1, 12), (3, 7), (4, 6), (3, 13), (2, 8),),
+    "x3": ((2, 12),),
+    "end": ((2, 9), (4, 7), (2, 10), (3, 8), (3, 9), (2, 11), (3, 10), (4, 8), (3, 12), (4, 9), (3, 11), (4, 10), (4, 12), (4, 11),),
+}
 MESH = pl.DeviceIdType.MESH
 f32 = jnp.float32
 bf16 = jnp.bfloat16
@@ -42,16 +80,9 @@
 
 
 def gelu_both(v):
-    density = jnp.exp(v * v * -0.5)
-    t = 1.0 / (1.0 + jnp.abs(v) * (0.3275911 / math.sqrt(2.0)))
-    poly = 0.5 * 1.061405429
-    poly = poly * t + 0.5 * -1.453152027
-    poly = poly * t + 0.5 * 1.421413741
-    poly = poly * t + 0.5 * -0.284496736
-    poly = poly * t + 0.5 * 0.254829592
-    tail = poly * t * density
-    below = jnp.where(v >= 0.0, 1.0 - tail, tail)
-    return v * below, below + v * density * (1.0 / math.sqrt(2.0 * math.pi))
+    below = 0.5 + 0.5 * lax.erf(v * (1.0 / math.sqrt(2.0)))
+    density = jnp.exp(v * v * -0.5) * (1.0 / math.sqrt(2.0 * math.pi))
+    return v * below, below + v * density
 
 
 def norm_stats(values):
@@ -81,18 +112,18 @@
     return jnp.sum(values, axis=0, keepdims=True)
 
 
-SMALL = ("ab", "mb", "g1", "h1", "eb", "rb", "g2", "h2", "post", "cnt")
-INPUTS = ("tok_hbm", "wa_hbm", "wm_hbm", "we_hbm", "wr_hbm", "cot_hbm") + tuple(k + "_hbm" for k in SMALL)
-OUTPUTS = ("act_hbm", "loss", "dx_hbm", "dwa_hbm", "dwm_hbm", "dwe_hbm", "dwr_hbm", "dab", "dmb", "dg1", "dh1", "deb", "drb", "dg2", "dh2")
-
-
-def layer_kernel(n, rows, ff, names, *refs):
-    r = dict(zip(names, refs, strict=True))
-    wm, we, wr, tok, pk, att_t = (r[k] for k in ("wm", "we", "wr", "tok", "pk", "att_t"))
-    low1, n1, fb, hid, gp, cot = (r[k] for k in ("low1", "n1", "fb", "hid", "gp", "cot"))
-    lse, s1, s2, mask, red = (r[k] for k in ("lse", "s1", "s2", "mask", "red"))
-    stage32, cls, vec, vec_out = (r[k] for k in ("stage32", "cls", "vec", "vec_out"))
-    ab, mb, g1, h1, eb, rb, g2, h2 = (r[k] for k in ("ab", "mb", "g1", "h1", "eb", "rb", "g2", "h2"))
+def colsum_low(values):
+    return dot_nn(jnp.ones((8, values.shape[0]), values.dtype), values)[0:1]
+
+
+def layer_kernel(n, rows, ff, names, small_count, *refs):
+    r = SimpleNamespace(**dict(zip(names, refs, strict=True)))
+    wm, we, wr, tok, pk, att_t = r.wm, r.we, r.wr, r.tok, r.pk, r.att_t
+    low1, n1, fb, hid, gp, cot = r.low1, r.n1, r.fb, r.hid, r.gp, r.cot
+    lse, s1, s2, mask, red = r.lse, r.s1, r.s2, r.mask, r.red
+    stage32, cls, vec, vec_out = r.stage32, r.cls, r.vec, r.vec_out
+    ab, mb, g1, h1, eb, rb, g2, h2 = r.ab, r.mb, r.g1, r.h1, r.eb, r.rb, r.g2, r.h2
+    small = list(zip(refs[6 : 6 + small_count], (ab, mb, g1, h1, eb, rb, g2, h2, r.post, r.cnt), strict=True))
     nz = n // 4
     part = D // n
     half = D // 2
@@ -110,8 +141,9 @@
     sibling = {"dp": z * 4 + x * 2 + (1 - c)}
     across = {"dp": z * 4 + (1 - x) * 2 + c}
     other_pair = {"pair": 1 - y}
+    slanted = {"pair": 1 - y, "dp": z * 4 + (1 - x) * 2 + c}
     along = [{"dp": ((z + k) % nz) * 4 + x * 2 + c} for k in range(1, nz)]
-    partners = [sibling, across, other_pair] + along
+    partners = [sibling, across, other_pair, slanted] + along
     barrier = pltpu.get_barrier_semaphore()
     for partner in partners:
         pl.semaphore_signal(barrier, inc=1, device_id=partner, device_id_type=MESH)
@@ -129,23 +161,23 @@
     loads = {}
 
     def load(key, source, target):
-        loads[key] = pltpu.make_async_copy(source, target, r["load_sem"].at[len(loads)])
+        loads[key] = pltpu.make_async_copy(source, target, r.load_sem.at[len(loads)])
         loads[key].start()
 
-    load("tok", r["tok_hbm"], tok)
+    load("tok", r.tok_hbm, tok)
     for j in range(3):
         for k in range(thirds):
             load(
                 ("wa", j, k),
-                r["wa_hbm"].at[:, pl.ds(j * D + k * SEQ, SEQ)],
+                r.wa_hbm.at[:, pl.ds(j * D + k * SEQ, SEQ)],
                 red.at[j, pl.ds(k * D, D), :],
             )
-    for key in SMALL:
-        load(key, r[key + "_hbm"], r[key])
-    load("wm", r["wm_hbm"], wm)
-    load("we", r["we_hbm"], we)
-    load("wr", r["wr_hbm"], wr)
-    load("cot", r["cot_hbm"], cot)
+    for k, (source, target) in enumerate(small):
+        load(k, source, target)
+    load("wm", r.wm_hbm, wm)
+    load("we", r.we_hbm, we)
+    load("wr", r.wr_hbm, wr)
+    load("cot", r.cot_hbm, cot)
 
     row_id = lax.broadcasted_iota(jnp.int32, (SEQ, SEQ), 0)
     col_id = lax.broadcasted_iota(jnp.int32, (SEQ, SEQ), 1)
@@ -176,8 +208,8 @@
         lax.fori_loop(first, last, step, 0)
 
     loads["tok"].wait()
-    for key in SMALL:
-        loads[key].wait()
+    for k in range(small_count):
+        loads[k].wait()
     for j in range(3):
         for k in range(thirds):
             loads[("wa", j, k)].wait()
@@ -197,30 +229,68 @@
 
     loop(0, blocks, project)
 
-    def attend_pair(b, h):
-        at = block_rows(b)
-        lanes = wide(h)
-        key_pair = pk[1, at, lanes]
-        value_t = pk[2, at, lanes].T
-        mixed = []
-        for s, query in enumerate(split_heads(pk[0, at, lanes])):
-            scores = dot_nt(key_pair, query) + mask[...]
-            peak = jnp.max(scores, axis=0, keepdims=True)
-            weight = jnp.exp(scores - peak)
-            total = jnp.sum(weight, axis=0, keepdims=True)
-            lse[2 * (b * PAIRS + h) + s] = peak + jnp.log(total)
-            out = dot_nn(value_t[s * HEAD : (s + 1) * HEAD], weight.astype(bf16))
-            mixed.append(out * (1.0 / total))
-        att_t[wide(h), block_lanes(b)] = jnp.concatenate(mixed, axis=0).astype(bf16)
-
     def attend(i):
         per = PAIRS // TOGETHER
-        for k in range(TOGETHER):
-            attend_pair(i // per, (i % per) * TOGETHER + k)
+        b = i // per
+        at = block_rows(b)
+        pairs = [(i % per) * TOGETHER + k for k in range(TOGETHER)]
+        scores = []
+        for h in pairs:
+            key_pair = pk[1, at, wide(h)]
+            scores += [dot_nt(key_pair, query) for query in split_heads(pk[0, at, wide(h)])]
+        weights = []
+        scales = []
+        for k, score in enumerate(scores):
+            score = score + mask[...]
+            peak = jnp.max(score, axis=0, keepdims=True)
+            weight = jnp.exp(score - peak)
+            total = jnp.sum(weight, axis=0, keepdims=True)
+            lse[2 * (b * PAIRS + pairs[k // 2]) + k % 2] = peak + jnp.log(total)
+            weights.append(weight.astype(bf16))
+            scales.append(1.0 / total)
+        for k, h in enumerate(pairs):
+            value_t = pk[2, at, wide(h)].T
+            mixed = [
+                dot_nn(value_t[s * HEAD : (s + 1) * HEAD], weights[2 * k + s]) * scales[2 * k + s] for s in range(2)
+            ]
+            att_t[wide(h), block_lanes(b)] = jnp.concatenate(mixed, axis=0).astype(bf16)
 
     loop(0, blocks * (PAIRS // TOGETHER), attend)
 
-    loads["wm"].wait()
+    def feed_chunk(here, j):
+        inner = dot_nn(here, we[:, j * D : (j + 1) * D]) + eb[:, j * D : (j + 1) * D]
+        hidden, slope = gelu_both(inner)
+        hidden = hidden.astype(bf16)
+        return hidden, slope, dot_nn(hidden, wr[j * D : (j + 1) * D, :])
+
+    for key in ("wm", "we", "wr"):
+        loads[key].wait()
+    picks = lax.broadcasted_iota(jnp.int32, (extra, rows), 1) == QLEN * lax.broadcasted_iota(
+        jnp.int32, (extra, rows), 0
+    )
+    first_attended = dot_nt(jnp.where(picks, 1.0, 0.0).astype(bf16), att_t[...]).astype(bf16)
+    for k in range(extra):
+        stage32[k : k + 1, :] = tok[k * QLEN : k * QLEN + 16, :].astype(f32)[0:1, :]
+    first_rows = norm_stats(stage32[0:extra, :] + (dot_nn(first_attended, wm[...]) + mb[...]))[0] * g1[...] + h1[...]
+    first_low = first_rows.astype(bf16)
+    leading = rb[...]
+    for j in range(ffc):
+        leading = leading + feed_chunk(first_low, j)[2]
+    leading = norm_stats(first_rows + leading)[0] * g2[...] + h2[...]
+    slot = ((c * 2 + y) * 2 + x) * nz + z
+    cls[pl.ds(pl.multiple_of(slot * extra, extra), extra), :] = leading.astype(bf16)
+
+    def gather(stage, first, count, device):
+        part_of = cls.at[pl.ds(pl.multiple_of(first * extra, extra), count * extra), :]
+        return remote(part_of, part_of, r.ag_send.at[stage], r.ag_recv.at[stage], device)
+
+    pl.semaphore_wait(barrier, len(partners))
+    gather_z = [gather(k, slot, 1, along[k]) for k in range(nz - 1)]
+    line = ((c * 2 + y) * 2 + x) * nz
+    gather_plane = [gather(nz - 1 + k, line, nz, to) for k, to in enumerate((across, other_pair, slanted))]
+    gather_core = gather(nz + 2, c * 4 * nz, 4 * nz, sibling)
+    for copy in gather_z:
+        copy.start()
 
     def merge(b):
         at = block_rows(b)
@@ -234,8 +304,6 @@
 
     loop(0, blocks, merge)
 
-    loads["we"].wait()
-    loads["wr"].wait()
 
     def act_stage(b, k):
         return red.at[k, block_rows(b), :]
@@ -244,25 +312,17 @@
         return [
             pltpu.make_async_copy(
                 act_stage(b, k),
-                r["act_hbm"].at[block_rows(b), pl.ds(k * SEQ, SEQ)],
-                r["act_sem"].at[b, k],
+                r.act_hbm.at[block_rows(b), pl.ds(k * SEQ, SEQ)],
+                r.act_sem.at[b, k],
             )
             for k in range(thirds)
         ]
 
-    def feed_chunk(here, j):
-        inner = dot_nn(here, we[:, j * D : (j + 1) * D]) + eb[:, j * D : (j + 1) * D]
-        hidden, slope = gelu_both(inner)
-        hidden = hidden.astype(bf16)
-        return hidden, slope, dot_nn(hidden, wr[j * D : (j + 1) * D, :])
-
-    def feed(b, halfway=None):
+    def feed(b):
         at = block_rows(b)
         here = low1[at, :]
         total = rb[...]
         for j in range(ffc):
-            if j == ffc // 2 and halfway is not None:
-                halfway()
             hidden, slope, out = feed_chunk(here, j)
             hid[j, :, block_lanes(b)] = hidden.T
             gp[j, at, :] = slope.astype(bf16)
@@ -276,29 +336,6 @@
         for copy in act_copies(b):
             copy.start()
 
-    for k in range(extra):
-        stage32[k : k + 1, :] = fb[k * QLEN : k * QLEN + 1, :]
-    slot = ((c * 2 + y) * 2 + x) * nz + z
-    first_rows = stage32[0:extra, :]
-    first_low = first_rows.astype(bf16)
-    leading = rb[...]
-    for j in range(ffc):
-        leading = leading + feed_chunk(first_low, j)[2]
-    leading = norm_stats(first_rows + leading)[0] * g2[...] + h2[...]
-    cls[pl.ds(pl.multiple_of(slot * extra, extra), extra), :] = leading.astype(bf16)
-
-    def gather(stage, first, count, device):
-        part_of = cls.at[pl.ds(pl.multiple_of(first * extra, extra), count * extra), :]
-        return remote(part_of, part_of, r["ag_send"].at[stage], r["ag_recv"].at[stage], device)
-
-    pl.semaphore_wait(barrier, len(partners))
-    gather_z = [gather(k, slot, 1, along[k]) for k in range(nz - 1)]
-    gather_x = gather(nz - 1, ((c * 2 + y) * 2 + x) * nz, nz, across)
-    gather_y = gather(nz, (c * 2 + y) * 2 * nz, 2 * nz, other_pair)
-    gather_c = [gather(nz + 1 + e, (c * 2 + [y, 1 - y][e]) * 2 * nz, 2 * nz, sibling) for e in range(2)]
-    for copy in gather_z:
-        copy.start()
-
     def feed_next(b):
         feed(b)
 
@@ -306,22 +343,17 @@
         def _():
             for copy in gather_z:
                 copy.wait()
-            gather_x.start()
-
-        @pl.when(b == 1)
+            for copy in gather_plane:
+                copy.start()
+
+        @pl.when(b == 2)
         def _():
-            gather_x.wait()
-            gather_y.start()
-            gather_c[0].start()
-
-    def last_gather():
-        gather_y.wait()
-        gather_c[1].start()
-
-    loop(0, blocks - 1, feed_next)
-    feed(blocks - 1, last_gather)
-    gather_c[0].wait()
-    gather_c[1].wait()
+            for copy in gather_plane:
+                copy.wait()
+            gather_core.start()
+
+    loop(0, blocks, feed_next)
+    gather_core.wait()
 
     nq = n * extra
     spare = blocks * SEQ
@@ -346,7 +378,7 @@
     real = place % (PLEN // QLEN) == 0
     listed = jnp.zeros((nq, nq), jnp.int32)
     for k in range(KPOS):
-        wanted = jnp.where(r["cnt"][...] > k, r["post"][k : k + 1, :], -1)
+        wanted = jnp.where(r.cnt[...] > k, r.post[k : k + 1, :], -1)
         listed = jnp.where(number == wanted, 1, listed)
     listed = (listed == 1) & real
     all_scores = jnp.where(real, match, negative)
@@ -357,7 +389,7 @@
     live_peak = jnp.max(live_scores, axis=0, keepdims=True)
     live_total = jnp.sum(jnp.where(listed, jnp.exp(live_scores - live_peak), 0.0), axis=0, keepdims=True)
     lse_live = live_peak + jnp.log(live_total)
-    r["loss"][...] = jnp.sum(lse_all - lse_live, axis=1, keepdims=True) * (1.0 / nq)
+    r.loss[...] = jnp.sum(lse_all - lse_live, axis=1, keepdims=True) * (1.0 / nq)
     grad_match = jnp.exp(all_scores - lse_all) - jnp.where(listed, jnp.exp(live_scores - lse_live), 0.0)
     grad_match = (loss_weight * grad_match).astype(bf16)
 
@@ -390,31 +422,37 @@
         low = grad.astype(bf16)
         fb[at, :] = grad
         cot[at, :] = low
-        vec[5 + ffc : 6 + ffc, :] += colsum(low.astype(f32))
+        vec[5 + ffc : 6 + ffc, :] += colsum_low(low)
         vec[6 + ffc : 7 + ffc, :] += colsum(upstream * normed)
         vec[7 + ffc : 8 + ffc, :] += colsum(upstream)
 
     loop(0, blocks, second_back)
 
-    units = (
-        [(red, k, shard, "r", k) for k in range(thirds)]
-        + [(hid, j, part, "w", j) for j in range(ffc)]
-        + [(gp, j, part, "w", ffc + j) for j in range(4)]
-    )
-    unit_out = (
-        [r["dwr_hbm"].at[:, pl.ds(k * SEQ, SEQ)] for k in range(thirds)]
-        + [r["dwe_hbm"].at[:, pl.ds(j * D, D)] for j in range(ffc)]
-        + [r["dwm_hbm"]]
-        + [r["dwa_hbm"].at[:, pl.ds(j * D, D)] for j in range(3)]
-    )
+    units = []
+    unit_out = []
+
+    def leave(ref, j, kind, at, width, out, first, pieces):
+        for k in range(pieces):
+            piece = width // pieces
+            units.append((ref, j, part if kind else shard, kind, at, k * piece, piece))
+            unit_out.append(out.at[:, pl.ds(first + k * piece, piece)])
+
+    for k in range(thirds):
+        leave(red, k, 0, k, SEQ, r.dwr_hbm, k * SEQ, PIECES[k])
+    for j in range(ffc):
+        leave(hid, j, 1, j, D, r.dwe_hbm, j * D, PIECES[thirds + j])
+    leave(gp, 0, 1, ffc, D, r.dwm_hbm, 0, PIECES[thirds + ffc])
+    for j in range(3):
+        leave(gp, 1 + j, 1, ffc + 1 + j, D, r.dwa_hbm, j * D, PIECES[thirds + ffc + 1 + j])
+    landing = ((r.recv_cr, r.recv_xr, r.recv_zr), (r.recv_cw, r.recv_xw, r.recv_zw))
 
     def unit_rows(u, first, count):
-        ref, j, each, kind, _ = units[u]
-        at = pl.ds(pl.multiple_of(first * each, each), count * each)
-        return ref.at[j, at, :] if kind == "r" else ref.at[j, at, pl.ds(0, D)]
+        ref, j, each, _, _, column, width = units[u]
+        return ref.at[j, pl.ds(pl.multiple_of(first * each, each), count * each), pl.ds(column, width)]
 
     def arrived(u, stage):
-        return r["recv_" + stage + units[u][3]].at[units[u][4]]
+        _, _, _, kind, at, column, width = units[u]
+        return landing[kind][stage].at[at, :, pl.ds(column, width)]
 
     def add_rows(u, first, source, source_first, count):
         each = units[u][2]
@@ -429,119 +467,251 @@
     def core_copy(u):
         return remote(
             unit_rows(u, (1 - c) * (n // 2), n // 2),
-            arrived(u, "c"),
-            r["c_send"].at[u],
-            r["c_recv"].at[u],
+            arrived(u, 0),
+            r.c_send.at[u],
+            r.c_recv.at[u],
             sibling,
         )
 
-    def across_copy(u):
+    here = c * (n // 2) + x * nz
+    there = c * (n // 2) + (1 - x) * nz
+    mate = z + 1 - 2 * (z % 2)
+    far = 2 - 2 * (z // 2)
+    outer = (z == 0) | (z == 3)
+    skip = 1 - z // 2
+    mate_at = {"dp": mate * 4 + x * 2 + c}
+    far_at = [{"dp": (far + k) * 4 + x * 2 + c} for k in range(2)]
+
+    def across_copy(u, k, first, count):
         return remote(
-            unit_rows(u, c * (n // 2) + (1 - x) * nz, nz),
-            arrived(u, "x"),
-            r["x_send"].at[u],
-            r["x_recv"].at[u],
+            unit_rows(u, there + first, count),
+            arrived(u, 1).at[shards_of(u, first, count), :],
+            r.x_send.at[u, k],
+            r.x_recv.at[u, k],
             across,
         )
 
+    def across_copies(u):
+        if MODES[u] == "a":
+            return [across_copy(u, 0, 0, nz)]
+        return [across_copy(u, 0, far, 2), across_copy(u, 1, z, 1)]
+
+    def shards_of(u, first, count):
+        each = units[u][2]
+        return pl.ds(pl.multiple_of(first * each, each), count * each)
+
+    def line_copy(u, k, source, count, slot, device, arrival=None):
+        return remote(
+            unit_rows(u, source, count),
+            arrived(u, 2).at[shards_of(u, slot, count), :],
+            r.z_send.at[u, k],
+            r.z_recv.at[u, k if arrival is None else arrival],
+            device,
+        )
+
+    def end_copy(u):
+        return line_copy(u, 0, here + skip, 3, 0, mate_at)
+
+    def inner_copy(u):
+        return line_copy(u, 0, here + mate, 1, 0, mate_at)
+
+    def middle_copies(u):
+        return [line_copy(u, 1 + k, here + far + k, 1, 3, far_at[k], 1) for k in range(2)]
+
+    def early_copy(u):
+        return line_copy(u, 3, there + mate, 1, 3, mate_at)
+
     def along_copy(u, k):
-        return remote(
-            unit_rows(u, c * (n // 2) + x * nz + (z + k) % nz, 1),
-            arrived(u, "z").at[k - 1],
-            r["z_send"].at[u, k - 1],
-            r["z_recv"].at[u, k - 1],
-            along[k - 1],
-        )
+        return line_copy(u, k - 1, here + (z + k) % nz, 1, k - 1, along[k - 1])
 
     def out_stage(u):
-        _, _, each, kind, at = units[u]
-        return r["stage_r" if kind == "r" else "stage32"].at[pl.ds(at * each, each), :]
+        _, _, each, kind, at, column, width = units[u]
+        return (stage32 if kind else r.stage_r).at[pl.ds(at * each, each), pl.ds(column, width)]
 
     def out_copy(u):
-        return pltpu.make_async_copy(out_stage(u), unit_out[u], r["out_sem"].at[u])
+        return pltpu.make_async_copy(out_stage(u), unit_out[u], r.out_sem.at[u])
 
     @scoped
     def core_start(u):
         core_copy(u).start()
 
     @scoped
-    def across_start(u):
+    def leave_core(u):
         core_copy(u).wait_recv()
-        add_rows(u, c * (n // 2) + (1 - x) * nz, arrived(u, "c"), (1 - x) * nz, nz)
-        across_copy(u).start()
-        add_rows(u, c * (n // 2) + x * nz, arrived(u, "c"), x * nz, nz)
+        if MODES[u] == "a":
+            add_rows(u, there, arrived(u, 0), (1 - x) * nz, nz)
+            across_copies(u)[0].start()
+        else:
+            add_rows(u, there + mate, arrived(u, 0), (1 - x) * nz + mate, 1)
+            early_copy(u).start()
+            add_rows(u, there + far, arrived(u, 0), (1 - x) * nz + far, 2)
+            across_copies(u)[0].start()
+            add_rows(u, there + z, arrived(u, 0), (1 - x) * nz + z, 1)
+        add_rows(u, here, arrived(u, 0), x * nz, nz)
 
     @scoped
-    def along_start(u):
-        across_copy(u).wait_recv()
-        add_rows(u, c * (n // 2) + x * nz, arrived(u, "x"), 0, nz)
-        for k in range(1, nz):
-            along_copy(u, k).start()
+    def second_step(u):
+        if MODES[u] == "a":
+            across_copies(u)[0].wait_recv()
+            add_rows(u, here, arrived(u, 1), 0, nz)
+
+            @pl.when(outer)
+            def _():
+                end_copy(u).start()
+
+            @pl.when(jnp.logical_not(outer))
+            def _():
+                inner_copy(u).start()
+        else:
+            early_copy(u).wait_recv()
+            add_rows(u, there + z, arrived(u, 2), 3, 1)
+            across_copies(u)[1].start()
+
+    @scoped
+    def third_step(u):
+        if MODES[u] == "a":
+
+            @pl.when(jnp.logical_not(outer))
+            def _():
+                end_copy(u).wait_recv()
+                add_rows(u, here + skip, arrived(u, 2), 0, 3)
+                for copy in middle_copies(u):
+                    copy.start()
+        else:
+            for copy in across_copies(u):
+                copy.wait_recv()
+            add_rows(u, here + far, arrived(u, 1), far, 2)
+            add_rows(u, here + z, arrived(u, 1), z, 1)
+            for k in range(1, nz):
+                along_copy(u, k).start()
 
     @scoped
     def finish(u):
-        total = unit_rows(u, c * (n // 2) + x * nz + z, 1)[...].astype(f32)
+        def landed(slot):
+            return arrived(u, 2)[shards_of(u, slot, 1), :].astype(f32)
+
+        own = unit_rows(u, here + z, 1)
+        if MODES[u] == "a":
+            middle_copies(u)[0].wait_recv()
+            out_stage(u)[...] = own[...].astype(f32) + landed(3)
+
+            @pl.when(outer)
+            def _():
+                inner_copy(u).wait_recv()
+                out_stage(u)[...] += landed(0)
+        else:
+            total = own[...].astype(f32)
+            for k in range(1, nz):
+                along_copy(u, k).wait_recv()
+                total = total + landed(k - 1)
+            out_stage(u)[...] = total
+        out_copy(u).start()
+
+    def vec_part(first, count):
+        return vec_out.at[pl.ds(first, count)]
+
+    mine = c * (n // 2) + x * nz
+    vec_c = remote(
+        vec_part((1 - c) * (n // 2), n // 2), r.vec_c, r.v_send.at[0], r.v_recv.at[0], sibling
+    )
+    vec_x = remote(
+        vec_part(c * (n // 2) + (1 - x) * nz, nz), r.vec_x, r.v_send.at[1], r.v_recv.at[1], across
+    )
+    vec_z = [
+        remote(
+            vec_part(mine + (z + k) % nz, 1),
+            r.vec_z.at[pl.ds(k - 1, 1)],
+            r.v_send.at[1 + k],
+            r.v_recv.at[1 + k],
+            along[k - 1],
+        )
+        for k in range(1, nz)
+    ]
+    def vec_start():
+        vec_c.start()
+
+    def vec_leave_core():
+        vec_c.wait()
+        vec_out[pl.ds(c * (n // 2), n // 2)] += r.vec_c[...]
+        vec_x.start()
+
+    def vec_leave_plane():
+        vec_x.wait()
+        vec_out[pl.ds(mine, nz)] += r.vec_x[...]
+        for copy in vec_z:
+            copy.start()
+
+    def vec_finish():
+        for copy in vec_z:
+            copy.wait()
+        total = vec_out[mine + z]
         for k in range(1, nz):
-            along_copy(u, k).wait_recv()
-            total = total + arrived(u, "z")[k - 1].astype(f32)
-        out_stage(u)[...] = total
-        out_copy(u).start()
+            total = total + r.vec_z[k - 1]
+        for e in range(2):
+            r.dab[:, e * part : (e + 1) * part] = total[e : e + 1, 0:part]
+        for e in range(ffc):
+            r.deb[:, e * part : (e + 1) * part] = total[5 + e : 6 + e, 0:part]
+        for out, row in ((r.dmb, 2), (r.dg1, 3), (r.dh1, 4), (r.drb, 5 + ffc), (r.dg2, 6 + ffc), (r.dh2, 7 + ffc)):
+            out[...] = total[row : row + 1, 0:part]
+
+    steps = (core_start, leave_core, second_step, third_step, finish)
+    vec_steps = (vec_start, vec_leave_core, vec_leave_plane, vec_finish)
+
+    def tick(name):
+        for step, u in SCHEDULE.get(name, ()):
+            if u == len(units):
+                vec_steps[step]()
+            else:
+                steps[step](u)
+
+    def ticks_at(name, count, i):
+        for k in range(count):
+            if name + str(k) in SCHEDULE:
+                pl.when(i == k)(partial(tick, name + str(k)))
 
     def spot(d):
         return ((d % 2) * 2 + (d // 2) % 2) * nz + d // 4
 
-    def spread(u, result, first):
+    def spread(ref, j, result, first):
         for d in range(first, first + result.shape[0] // part):
             piece = result[(d - first) * part : (d - first + 1) * part]
-            unit_rows(u, spot(d), 1)[...] = piece.astype(bf16)
+            ref[j, spot(d) * part : (spot(d) + 1) * part, 0:D] = piece.astype(bf16)
 
     for b in range(blocks):
         for copy in act_copies(b):
             copy.wait()
     for u in range(thirds):
 
-        def reduce_grad(t, u=u):
-            tiles = D // (2 * shard)
-            left = hid[t // tiles, pl.ds(pl.multiple_of((t % tiles) * 2 * shard, 16), 2 * shard), :]
+        def reduce_grad(i, u=u):
+            left = hid[pl.ds(i * 1, 1)].reshape(1 * D, rows)
             result = dot_nn(left, cot[:, u * SEQ : (u + 1) * SEQ]).astype(bf16)
-            for cc in range(2):
-                unit_rows(u, (cc * 2 + t % 2) * nz + t // 2, 1)[...] = result[cc * shard : (cc + 1) * shard]
-
-        loop(0, n // 2, reduce_grad)
-        core_start(u)
-        if u > 0:
-            across_start(u - 1)
-    expand_at = thirds
-    merge_at = thirds + ffc
-    attend_at = merge_at + 1
-
+            for k in range(1 * D // shard):
+                d = i * (1 * D // shard) + k
+                to = pl.ds(pl.multiple_of((((k % 2) * 2 + (k // 2) % 2) * nz + d // 4) * shard, 16), shard)
+                red[u, to, :] = result[k * shard : (k + 1) * shard]
+            if u > 0:
+                ticks_at("r%d_" % u, ffc // 1, i)
+
+        loop(0, ffc // 1, reduce_grad)
+        tick("r%d" % u)
     for j in range(ffc):
 
         def inner_back(b, j=j):
-            at = block_rows(b)
+            at = pl.ds(pl.multiple_of(b * 2 * SEQ, 2 * SEQ), 2 * SEQ)
             grad_hidden = dot_nt(cot[at, :], wr[j * D : (j + 1) * D, :])
             low = (grad_hidden * gp[j, at, :].astype(f32)).astype(bf16)
             gp[j, at, :] = low
             vec[5 + j : 6 + j, :] += colsum(low.astype(f32))
             fb[at, :] += dot_nt(low, we[:, j * D : (j + 1) * D])
 
-        loop(0, blocks, inner_back)
-        if j == 1:
-            along_start(0)
-            across_start(2)
-        elif j == 2:
-            along_start(1)
-            across_start(expand_at)
+            ticks_at("i%d_" % j, blocks // 2, b)
+
+        loop(0, blocks // 2, inner_back)
         for t in range(2):
             left = low1[:, t * half : (t + 1) * half]
-            spread(expand_at + j, dot_tn(left, gp[j]), (n // 2) * t)
-        core_start(expand_at + j)
-        if j == 2:
-            finish(0)
-        elif j == 3:
-            along_start(2)
-            across_start(expand_at + 1)
-    load("wa_again", r["wa_hbm"], we.at[:, pl.ds(0, 3 * D)])
+            spread(hid, j, dot_tn(left, gp[j]), (n // 2) * t)
+        tick("e%d" % j)
+    load("wa_again", r.wa_hbm, we.at[:, pl.ds(0, 3 * D)])
 
     def first_back(b):
         at = block_rows(b)
@@ -551,67 +721,55 @@
         low = grad.astype(bf16)
         fb[at, :] = grad
         cot[at, :] = low
-        vec[2:3, :] += colsum(low.astype(f32))
+        vec[2:3, :] += colsum_low(low)
         vec[3:4, :] += colsum(upstream * normed)
         vec[4:5, :] += colsum(upstream)
         n1[at, :] = dot_nt(low, wm[...]).astype(bf16)
+        ticks_at("f", blocks, b)
 
     loop(0, blocks, first_back)
     for t in range(2):
-        spread(merge_at, dot_nn(att_t[t * half : (t + 1) * half, :], cot[...]), (n // 2) * t)
-    core_start(merge_at)
-    along_start(expand_at)
-    across_start(expand_at + 2)
-    finish(1)
+        spread(gp, 0, dot_nn(att_t[t * half : (t + 1) * half, :], cot[...]), (n // 2) * t)
+    tick("m")
 
     def attend_back(i):
-        b = i // PAIRS
-        h = i % PAIRS
+        per = PAIRS // BACK_TOGETHER
+        b = i // per
         at = block_rows(b)
-        lanes = wide(h)
-        key_pair = pk[1, at, lanes]
-        value_pair = pk[2, at, lanes]
-        key_t = key_pair.T
-        queries = split_heads(pk[0, at, lanes])
-        grads = split_heads(n1[at, lanes])
+        pairs = [(i % per) * BACK_TOGETHER + k for k in range(BACK_TOGETHER)]
+        queries = []
+        grads = []
+        scores = []
+        grad_probs = []
+        for h in pairs:
+            queries.append(split_heads(pk[0, at, wide(h)]))
+            grads.append(split_heads(n1[at, wide(h)]))
+            scores += [dot_nt(pk[1, at, wide(h)], query) for query in queries[-1]]
+            grad_probs += [dot_nt(pk[2, at, wide(h)], grad) for grad in grads[-1]]
         probs = []
         slopes = []
-        query_grads = []
-        for s in range(2):
-            prob = jnp.exp(dot_nt(key_pair, queries[s]) + mask[...] - lse[2 * i + s])
-            grad_prob = dot_nt(value_pair, grads[s])
-            mean = jnp.sum(prob * grad_prob, axis=0, keepdims=True)
-            slope = (prob * (grad_prob - mean)).astype(bf16)
+        for k in range(2 * BACK_TOGETHER):
+            prob = jnp.exp(scores[k] + mask[...] - lse[2 * (b * PAIRS + pairs[k // 2]) + k % 2])
+            mean = jnp.sum(prob * grad_probs[k], axis=0, keepdims=True)
+            slopes.append((prob * (grad_probs[k] - mean)).astype(bf16))
             probs.append(prob.astype(bf16))
-            slopes.append(slope)
-            query_grads.append(dot_nn(key_t[s * HEAD : (s + 1) * HEAD], slope))
-        grad_value = dot_nn(jnp.concatenate(probs, axis=1), jnp.concatenate(grads, axis=0)).astype(bf16)
-        grad_key = dot_nn(jnp.concatenate(slopes, axis=1), jnp.concatenate(queries, axis=0)).astype(bf16)
-        grad_query = (jnp.concatenate(query_grads, axis=0) * (1.0 / math.sqrt(HEAD))).T.astype(bf16)
-        pk[0, at, lanes] = grad_query
-        pk[1, at, lanes] = grad_key
-        pk[2, at, lanes] = grad_value
-        vec[0:1, lanes] += colsum(grad_query.astype(f32))
-        vec[1:2, lanes] += colsum(grad_value.astype(f32))
-
-        @pl.when(i == 7)
-        def _():
-            along_start(expand_at + 1)
-            across_start(expand_at + 3)
-            finish(2)
-
-        @pl.when(i == 14)
-        def _():
-            along_start(expand_at + 2)
-            across_start(merge_at)
-            finish(expand_at)
-
-        @pl.when(i == 21)
-        def _():
-            along_start(expand_at + 3)
-            finish(expand_at + 1)
-
-    loop(0, blocks * PAIRS, attend_back)
+        for k, h in enumerate(pairs):
+            lanes = wide(h)
+            both = slice(2 * k, 2 * k + 2)
+            key_t = pk[1, at, lanes].T
+            grad_value = dot_nn(jnp.concatenate(probs[both], axis=1), jnp.concatenate(grads[k], axis=0)).astype(bf16)
+            grad_key = dot_nn(jnp.concatenate(slopes[both], axis=1), jnp.concatenate(queries[k], axis=0)).astype(bf16)
+            grad_query = [dot_nn(key_t[s * HEAD : (s + 1) * HEAD], slopes[2 * k + s]) for s in range(2)]
+            grad_query = (jnp.concatenate(grad_query, axis=0) * (1.0 / math.sqrt(HEAD))).T.astype(bf16)
+            pk[0, at, lanes] = grad_query
+            pk[1, at, lanes] = grad_key
+            pk[2, at, lanes] = grad_value
+            vec[0:1, lanes] += colsum(grad_query.astype(f32))
+            vec[1:2, lanes] += colsum(grad_value.astype(f32))
+
+        ticks_at("t", blocks * per, i)
+
+    loop(0, blocks * (PAIRS // BACK_TOGETHER), attend_back)
 
     for d in range(n):
         def chunk(row, first, d=d):
@@ -627,50 +785,17 @@
         for e in range(ffc):
             vec_out[at, 5 + e : 6 + e, 0:part] = chunk(5, ffc * d + e)
 
-    def vec_part(first, count):
-        return vec_out.at[pl.ds(first, count)]
-
-    mine = c * (n // 2) + x * nz
-    vec_c = remote(
-        vec_part((1 - c) * (n // 2), n // 2), r["vec_c"], r["v_send"].at[0], r["v_recv"].at[0], sibling
-    )
-    vec_x = remote(
-        vec_part(c * (n // 2) + (1 - x) * nz, nz), r["vec_x"], r["v_send"].at[1], r["v_recv"].at[1], across
-    )
-    vec_z = [
-        remote(
-            vec_part(mine + (z + k) % nz, 1),
-            r["vec_z"].at[pl.ds(k - 1, 1)],
-            r["v_send"].at[1 + k],
-            r["v_recv"].at[1 + k],
-            along[k - 1],
-        )
-        for k in range(1, nz)
-    ]
-    vec_c.start()
+    tick("v")
 
     for j in range(3):
-        unit = attend_at + j
         for t in range(2):
-            spread(unit, dot_tn(tok[:, t * half : (t + 1) * half], pk[j]), (n // 2) * t)
-        core_start(unit)
-        if j == 0:
-            vec_c.wait()
-            vec_out[pl.ds(c * (n // 2), n // 2)] += r["vec_c"][...]
-            vec_x.start()
-        elif j == 1:
-            across_start(attend_at)
-            along_start(merge_at)
-            finish(expand_at + 2)
-            vec_x.wait()
-            vec_out[pl.ds(mine, nz)] += r["vec_x"][...]
-            for copy in vec_z:
-                copy.start()
+            spread(gp, 1 + j, dot_tn(tok[:, t * half : (t + 1) * half], pk[j]), (n // 2) * t)
+        tick("a%d" % j)
 
     loads["wa_again"].wait()
 
     def dx_copy(b):
-        return pltpu.make_async_copy(tok.at[block_rows(b), :], r["dx_hbm"].at[block_rows(b), :], r["dx_sem"].at[b])
+        return pltpu.make_async_copy(tok.at[block_rows(b), :], r.dx_hbm.at[block_rows(b), :], r.dx_sem.at[b])
 
     def token_grad(b):
         at = block_rows(b)
@@ -680,39 +805,29 @@
         tok[at, :] = total.astype(bf16)
         dx_copy(b).start()
 
-        @pl.when(b == 0)
-        def _():
-            across_start(attend_at + 1)
-            finish(expand_at + 3)
-
-        @pl.when(b == 3)
-        def _():
-            along_start(attend_at)
-            across_start(attend_at + 2)
-            finish(merge_at)
+        ticks_at("x", blocks, b)
 
     loop(0, blocks, token_grad)
-    for copy in vec_z:
-        copy.wait()
-    total = vec_out[mine + z]
-    for k in range(1, nz):
-        total = total + r["vec_z"][k - 1]
-    for e in range(2):
-        r["dab"][:, e * part : (e + 1) * part] = total[e : e + 1, 0:part]
-    for e in range(ffc):
-        r["deb"][:, e * part : (e + 1) * part] = total[5 + e : 6 + e, 0:part]
-    for key, row in (("dmb", 2), ("dg1", 3), ("dh1", 4), ("drb", 5 + ffc), ("dg2", 6 + ffc), ("dh2", 7 + ffc)):
-        r[key][...] = total[row : row + 1, 0:part]
-    along_start(attend_at + 1)
-    finish(attend_at)
-    along_start(attend_at + 2)
-    finish(attend_at + 1)
-    finish(attend_at + 2)
+    tick("end")
     for u in range(len(units)):
         core_copy(u).wait_send()
-        across_copy(u).wait_send()
-        for k in range(1, nz):
-            along_copy(u, k).wait_send()
+        for copy in across_copies(u):
+            copy.wait_send()
+        if MODES[u] == "a":
+
+            @pl.when(outer)
+            def _(u=u):
+                end_copy(u).wait_send()
+
+            @pl.when(jnp.logical_not(outer))
+            def _(u=u):
+                inner_copy(u).wait_send()
+                for copy in middle_copies(u):
+                    copy.wait_send()
+        else:
+            early_copy(u).wait_send()
+            for k in range(1, nz):
+                along_copy(u, k).wait_send()
         out_copy(u).wait()
     for b in range(blocks):
         dx_copy(b).wait()
@@ -744,12 +859,25 @@
     extra = rows // QLEN
     blocks = rows // SEQ
     wide_units = ffc + 4
-    units = thirds + wide_units
+    units = sum(PIECES)
     wa, wm, we, wr = (args[k][0] for k in (1, 3, 7, 9))
-    small = [args[k] for k in (2, 4, 5, 6, 8, 10, 11, 12)] + [args[14].T, args[15][None, :]]
+    small = dict(
+        ab=args[2],
+        mb=args[4],
+        g1=args[5],
+        h1=args[6],
+        eb=args[8],
+        rb=args[10],
+        g2=args[11],
+        h2=args[12],
+        post=args[14].T,
+        cnt=args[15][None, :],
+    )
+    given = dict(tok_hbm=tokens, wa_hbm=wa, wm_hbm=wm, we_hbm=we, wr_hbm=wr, cot_hbm=cotangent)
+    given.update({k + "_hbm": v for k, v in small.items()})
     dma = pltpu.SemaphoreType.DMA
     scratch = dict(
-        zip(SMALL, [pltpu.VMEM(value.shape, value.dtype) for value in small], strict=True),
+        {k: pltpu.VMEM(v.shape, v.dtype) for k, v in small.items()},
         wm=pltpu.VMEM((D, D), bf16),
         we=pltpu.VMEM((D, ff), bf16),
         wr=pltpu.VMEM((ff, D), bf16),
@@ -777,56 +905,58 @@
         vec_z=pltpu.VMEM((nz - 1, 16, 128), f32),
         recv_cr=pltpu.VMEM((thirds, ff // 2, SEQ), bf16),
         recv_xr=pltpu.VMEM((thirds, ff // 4, SEQ), bf16),
-        recv_zr=pltpu.VMEM((thirds, nz - 1, shard, SEQ), bf16),
+        recv_zr=pltpu.VMEM((thirds, nz * shard, SEQ), bf16),
         recv_cw=pltpu.VMEM((wide_units, D // 2, D), bf16),
         recv_xw=pltpu.VMEM((wide_units, D // 4, D), bf16),
-        recv_zw=pltpu.VMEM((wide_units, nz - 1, part, D), bf16),
+        recv_zw=pltpu.VMEM((wide_units, nz * part, D), bf16),
         load_sem=dma((32,)),
         act_sem=dma((blocks, thirds)),
         dx_sem=dma((blocks,)),
         out_sem=dma((units,)),
         c_send=dma((units,)),
         c_recv=dma((units,)),
-        x_send=dma((units,)),
-        x_recv=dma((units,)),
-        z_send=dma((units, nz - 1)),
-        z_recv=dma((units, nz - 1)),
+        x_send=dma((units, 2)),
+        x_recv=dma((units, 2)),
+        z_send=dma((units, nz)),
+        z_recv=dma((units, nz)),
         ag_send=dma((nz + 3,)),
         ag_recv=dma((nz + 3,)),
         v_send=dma((nz + 1,)),
         v_recv=dma((nz + 1,)),
     )
-    names = list(INPUTS) + list(OUTPUTS) + list(scratch)
     hbm = pl.BlockSpec(memory_space=pl.ANY)
     near = pl.BlockSpec(memory_space=pltpu.VMEM)
     shape = jax.ShapeDtypeStruct
-    shapes = [
-        shape((rows, D), bf16),
-        shape((1, 1), f32),
-        shape((rows, D), bf16),
-        shape((part, 3 * D), f32),
-        shape((part, D), f32),
-        shape((part, ff), f32),
-        shape((ff // n, D), f32),
-        shape((1, 2 * part), f32),
-        shape((1, part), f32),
-        shape((1, part), f32),
-        shape((1, part), f32),
-        shape((1, ff // n), f32),
-        shape((1, part), f32),
-        shape((1, part), f32),
-        shape((1, part), f32),
-    ]
+    row_out = shape((1, part), f32)
+    wanted = dict(
+        act_hbm=shape((rows, D), bf16),
+        loss=shape((1, 1), f32),
+        dx_hbm=shape((rows, D), bf16),
+        dwa_hbm=shape((part, 3 * D), f32),
+        dwm_hbm=shape((part, D), f32),
+        dwe_hbm=shape((part, ff), f32),
+        dwr_hbm=shape((ff // n, D), f32),
+        dab=shape((1, 2 * part), f32),
+        dmb=row_out,
+        dg1=row_out,
+        dh1=row_out,
+        deb=shape((1, ff // n), f32),
+        drb=row_out,
+        dg2=row_out,
+        dh2=row_out,
+    )
+    shapes = list(wanted.values())
+    names = list(given) + list(wanted) + list(scratch)
     outs = pl.pallas_call(
-        partial(layer_kernel, n, rows, ff, names),
+        partial(layer_kernel, n, rows, ff, names, len(small)),
         out_shape=shapes,
-        in_specs=[hbm] * (6 + len(small)),
+        in_specs=[hbm] * len(given),
         out_specs=[hbm, near] + [hbm] * 5 + [near] * 8,
         scratch_shapes=list(scratch.values()),
         compiler_params=pltpu.CompilerParams(
             collective_id=0, has_side_effects=True, vmem_limit_bytes=VMEM_BYTES
         ),
-    )(tokens, wa, wm, we, wr, cotangent, *small)
+    )(*given.values())
     act, loss, dx, dwa, dwm, dwe, dwr, dab, dmb, dg1, dh1, deb, drb, dg2, dh2 = pl.pallas_call(
         partial(hand_over_kernel, len(shapes)),
         out_shape=shapes,
@@ -1156,6 +1286,6 @@
         P("pair", "dp"),
     )
     n = mesh.shape["dp"]
-    fits = mesh.shape["pair"] == 2 and n % 4 == 0 and D % n == 0 and (D // n) % 16 == 0
+    fits = mesh.shape["pair"] == 2 and n == 4 * LINE
     body = partial(fused_shards, n) if fits else shards
     return jax.shard_map(body, mesh=mesh, in_specs=in_specs, out_specs=out_specs, check_vma=False)

time: 161 us -> 136 us (0.84)
  Pallas kernels: 160 us -> 135 us
    pallas_call x1, Pallas kernels: 156 us -> 131 us  [fused_shards(): pl.pallas_call(partial(layer_kernel, n, rows, ff, names, len(small)), out...]
where the time goes in v2:
time: 136 us
  Pallas kernels  135 us (99%)
    pallas_call x1, Pallas kernels, fused_shards(): pl.pallas_call(partial(layer_kernel, n, rows, ff, names, len(small)), out...  131 us
    pallas_call x1, Pallas kernels, fused_shards(): pl.pallas_call(partial(hand_over_kernel, len(shapes)), out_shape=shapes,...  4.58 us

profile of v2, /device:TPU:0, one launch (start us, length us, event | category | flops | bytes accessed | tf_op | source)
XLA Modules:
  0.0 136.2 jit_solution(5809504945910546297)
XLA Ops:
  0.7 130.8 %shard_map.271 = (bf16[1024,768]{1,0:T(8,128)(2,1)}, f32[1,1]{1,0:T(1,128)}, bf16[1024,768]{1,0:T(8,128)(2,1)}, f32[48,2304]{1,0:T(8,128)}, f32[48,768]{1,0:T(8,...) custom-call(bf16[1024,768]{1,0:T(8,128)(2,1)} %bitcast.18, ...), custom_call_target="tpu_custom_call" | custom-call | tf_op jit(solution)/shard_map/pallas_call | solution.py:950
  131.4 4.6 %shard_map.272 = (bf16[1024,768]{1,0:T(8,128)(2,1)}, f32[1,1]{1,0:T(1,128)}, bf16[1024,768]{1,0:T(8,128)(2,1)}, f32[48,2304]{1,0:T(8,128)}, f32[48,768]{1,0:T(8,...) custom-call(bf16[1024,768]{1,0:T(8,128)(2,1)} %get-tuple-element.45., ...), custom_call_target="tpu_custom_call" | custom-call | tf_op jit(solution)/shard_map/pallas_call | solution.py:960

commit v3 on v2

--- a/solution.py
+++ b/solution.py
@@ -27,40 +27,40 @@
 TOGETHER = 6
 BACK_TOGETHER = 2
 LINE = 4
-PIECES = (1, 1, 1, 1, 1, 1, 1, 1, 1, 2, 2)
-MODES = "babbaaaaaaaab"
+PIECES = (1, 1, 1, 1, 1, 1, 1, 2, 2, 2, 2)
+MODES = "cdacacacadaacac"
 SCHEDULE = {
     "r0": ((0, 0),),
     "r1": ((0, 1),),
     "r2_0": ((1, 0),),
     "r2": ((0, 2), (1, 1),),
-    "i0_0": ((2, 0),),
     "i0_1": ((1, 2),),
     "e0": ((0, 3),),
-    "i1_1": ((2, 2), (1, 3),),
+    "i1_1": ((2, 0), (1, 3),),
     "e1": ((0, 4),),
-    "i2_0": ((2, 1), (2, 3),),
-    "i2_1": ((3, 0), (1, 4),),
+    "i2_1": ((1, 4),),
     "e2": ((0, 5),),
-    "i3_1": ((1, 5), (3, 2), (3, 1),),
+    "i3_0": ((2, 2),),
+    "i3_1": ((2, 1), (1, 5),),
     "e3": ((0, 6),),
-    "f1": ((3, 3),),
-    "f2": ((1, 6),),
-    "f3": ((4, 0),),
-    "m": ((0, 7),),
-    "t1": ((2, 4),),
-    "t2": ((1, 7), (4, 2),),
-    "t5": ((2, 5),),
-    "t6": ((4, 1),),
-    "t10": ((2, 6), (3, 4), (4, 3),),
-    "v": ((0, 13),),
-    "a0": ((0, 8), (3, 5), (1, 13),),
-    "a1": ((0, 9), (0, 10), (2, 7), (1, 8), (2, 13), (4, 4),),
-    "a2": ((0, 11), (0, 12), (3, 6), (1, 9), (1, 10), (4, 5),),
-    "x0": ((1, 11),),
-    "x2": ((1, 12), (3, 7), (4, 6), (3, 13), (2, 8),),
-    "x3": ((2, 12),),
-    "end": ((2, 9), (4, 7), (2, 10), (3, 8), (3, 9), (2, 11), (3, 10), (4, 8), (3, 12), (4, 9), (3, 11), (4, 10), (4, 12), (4, 11),),
+    "f0": ((2, 3),),
+    "f3": ((1, 6),),
+    "m": ((0, 7), (0, 8), (3, 2), (4, 0), (2, 4),),
+    "t1": ((4, 1),),
+    "t2": ((1, 7),),
+    "t3": ((4, 3),),
+    "t4": ((1, 8),),
+    "t5": ((2, 5), (3, 4),),
+    "t6": ((4, 2),),
+    "t10": ((2, 6),),
+    "v": ((0, 15), (4, 5), (2, 7),),
+    "a0": ((0, 9), (0, 10), (1, 15),),
+    "a1": ((0, 11), (0, 12), (2, 8), (1, 9), (2, 15), (3, 6), (1, 10), (4, 4),),
+    "a2": ((0, 13), (0, 14), (1, 11), (1, 12), (4, 7),),
+    "x0": ((1, 13), (3, 8), (1, 14),),
+    "x1": ((2, 10),),
+    "x3": ((2, 11),),
+    "end": ((2, 9), (3, 15), (4, 6), (2, 12), (3, 10), (4, 8), (2, 13), (3, 11), (4, 12), (2, 14), (4, 10), (4, 9), (3, 13), (4, 11), (4, 14), (4, 13),),
 }
 MESH = pl.DeviceIdType.MESH
 f32 = jnp.float32
@@ -492,9 +492,36 @@
         )
 
     def across_copies(u):
-        if MODES[u] == "a":
+        if MODES[u] == "d":
+            return [line_x_copy(u)]
+        if MODES[u] != "b":
             return [across_copy(u, 0, 0, nz)]
         return [across_copy(u, 0, far, 2), across_copy(u, 1, z, 1)]
+
+    def line_x_copy(u):
+        return remote(
+            unit_rows(u, there + z, 1),
+            arrived(u, 2).at[shards_of(u, 3, 1), :],
+            r.x_send.at[u, 3],
+            r.x_recv.at[u, 3],
+            across,
+        )
+
+    def line_copies(u):
+        copies = []
+        for k in range(1, nz):
+            to = (z + k) % nz
+            copies.append(along_copy(u, k))
+            copies.append(
+                remote(
+                    unit_rows(u, there + to, 1),
+                    arrived(u, 1).at[shards_of(u, k - 1, 1), :],
+                    r.x_send.at[u, k - 1],
+                    r.x_recv.at[u, k - 1],
+                    along[k - 1],
+                )
+            )
+        return copies
 
     def shards_of(u, first, count):
         each = units[u][2]
@@ -518,6 +545,7 @@
     def middle_copies(u):
         return [line_copy(u, 1 + k, here + far + k, 1, 3, far_at[k], 1) for k in range(2)]
 
+
     def early_copy(u):
         return line_copy(u, 3, there + mate, 1, 3, mate_at)
 
@@ -538,7 +566,12 @@
     @scoped
     def leave_core(u):
         core_copy(u).wait_recv()
-        if MODES[u] == "a":
+        if MODES[u] == "d":
+            add_rows(u, c * (n // 2), arrived(u, 0), 0, n // 2)
+            for copy in line_copies(u):
+                copy.start()
+            return
+        if MODES[u] != "b":
             add_rows(u, there, arrived(u, 0), (1 - x) * nz, nz)
             across_copies(u)[0].start()
         else:
@@ -562,6 +595,18 @@
             @pl.when(jnp.logical_not(outer))
             def _():
                 inner_copy(u).start()
+        elif MODES[u] == "d":
+            for copy in line_copies(u):
+                copy.wait_recv()
+            for k in range(nz - 1):
+                add_rows(u, there + z, arrived(u, 1), k, 1)
+                add_rows(u, here + z, arrived(u, 2), k, 1)
+            line_x_copy(u).start()
+        elif MODES[u] == "c":
+            across_copies(u)[0].wait_recv()
+            add_rows(u, here, arrived(u, 1), 0, nz)
+            for k in range(1, nz):
+                along_copy(u, k).start()
         else:
             early_copy(u).wait_recv()
             add_rows(u, there + z, arrived(u, 2), 3, 1)
@@ -591,7 +636,10 @@
             return arrived(u, 2)[shards_of(u, slot, 1), :].astype(f32)
 
         own = unit_rows(u, here + z, 1)
-        if MODES[u] == "a":
+        if MODES[u] == "d":
+            line_x_copy(u).wait_recv()
+            out_stage(u)[...] = own[...].astype(f32) + landed(3)
+        elif MODES[u] == "a":
             middle_copies(u)[0].wait_recv()
             out_stage(u)[...] = own[...].astype(f32) + landed(3)
 
@@ -813,7 +861,10 @@
         core_copy(u).wait_send()
         for copy in across_copies(u):
             copy.wait_send()
-        if MODES[u] == "a":
+        if MODES[u] == "d":
+            for copy in line_copies(u):
+                copy.wait_send()
+        elif MODES[u] == "a":
 
             @pl.when(outer)
             def _(u=u):
@@ -825,7 +876,8 @@
                 for copy in middle_copies(u):
                     copy.wait_send()
         else:
-            early_copy(u).wait_send()
+            if MODES[u] == "b":
+                early_copy(u).wait_send()
             for k in range(1, nz):
                 along_copy(u, k).wait_send()
         out_copy(u).wait()
@@ -915,8 +967,8 @@
         out_sem=dma((units,)),
         c_send=dma((units,)),
         c_recv=dma((units,)),
-        x_send=dma((units, 2)),
-        x_recv=dma((units, 2)),
+        x_send=dma((units, nz)),
+        x_recv=dma((units, nz)),
         z_send=dma((units, nz)),
         z_recv=dma((units, nz)),
         ag_send=dma((nz + 3,)),

time: 136 us -> 134 us (0.985)
  Pallas kernels: 135 us -> 133 us
    pallas_call x1, Pallas kernels: 131 us -> 128 us  [fused_shards(): pl.pallas_call(partial(layer_kernel, n, rows, ff, names, len(small)), out...]
where the time goes in v3:
time: 134 us
  Pallas kernels  133 us (99%)
    pallas_call x1, Pallas kernels, fused_shards(): pl.pallas_call(partial(layer_kernel, n, rows, ff, names, len(small)), out...  128 us
    pallas_call x1, Pallas kernels, fused_shards(): pl.pallas_call(partial(hand_over_kernel, len(shapes)), out_shape=shapes,...  4.58 us

profile of v3, /device:TPU:0, one launch (start us, length us, event | category | flops | bytes accessed | tf_op | source)
XLA Modules:
  0.0 133.8 jit_solution(8909851242501206832)
XLA Ops:
  0.7 128.3 %shard_map.271 = (bf16[1024,768]{1,0:T(8,128)(2,1)}, f32[1,1]{1,0:T(1,128)}, bf16[1024,768]{1,0:T(8,128)(2,1)}, f32[48,2304]{1,0:T(8,128)}, f32[48,768]{1,0:T(8,...) custom-call(bf16[1024,768]{1,0:T(8,128)(2,1)} %bitcast.18, ...), custom_call_target="tpu_custom_call" | custom-call | tf_op jit(solution)/shard_map/pallas_call | solution.py:1002
  129.0 4.6 %shard_map.272 = (bf16[1024,768]{1,0:T(8,128)(2,1)}, f32[1,1]{1,0:T(1,128)}, bf16[1024,768]{1,0:T(8,128)(2,1)}, f32[48,2304]{1,0:T(8,128)}, f32[48,768]{1,0:T(8,...) custom-call(bf16[1024,768]{1,0:T(8,128)(2,1)} %get-tuple-element.45., ...), custom_call_target="tpu_custom_call" | custom-call | tf_op jit(solution)/shard_map/pallas_call | solution.py:1012

commit v4 on v3

--- a/solution.py
+++ b/solution.py
@@ -41,26 +41,26 @@
     "i2_1": ((1, 4),),
     "e2": ((0, 5),),
     "i3_0": ((2, 2),),
-    "i3_1": ((2, 1), (1, 5),),
+    "i3_1": ((1, 5), (2, 1),),
     "e3": ((0, 6),),
-    "f0": ((2, 3),),
+    "f1": ((2, 3),),
     "f3": ((1, 6),),
-    "m": ((0, 7), (0, 8), (3, 2), (4, 0), (2, 4),),
-    "t1": ((4, 1),),
+    "m": ((0, 7), (0, 8), (3, 2), (4, 0),),
+    "t0": ((2, 4),),
     "t2": ((1, 7),),
-    "t3": ((4, 3),),
-    "t4": ((1, 8),),
-    "t5": ((2, 5), (3, 4),),
-    "t6": ((4, 2),),
-    "t10": ((2, 6),),
-    "v": ((0, 15), (4, 5), (2, 7),),
-    "a0": ((0, 9), (0, 10), (1, 15),),
-    "a1": ((0, 11), (0, 12), (2, 8), (1, 9), (2, 15), (3, 6), (1, 10), (4, 4),),
-    "a2": ((0, 13), (0, 14), (1, 11), (1, 12), (4, 7),),
-    "x0": ((1, 13), (3, 8), (1, 14),),
+    "t4": ((4, 3),),
+    "t5": ((2, 5), (1, 8),),
+    "t6": ((3, 4), (4, 1),),
+    "t7": ((4, 2),),
+    "t11": ((2, 6),),
+    "v": ((0, 15), (4, 5),),
+    "a0": ((0, 9), (0, 10), (2, 7), (1, 15),),
+    "a1": ((0, 11), (0, 12), (1, 9), (1, 10), (4, 4), (2, 8),),
+    "a2": ((0, 13), (0, 14), (2, 15), (3, 6), (1, 11), (1, 12),),
+    "x0": ((1, 13), (4, 7), (1, 14),),
     "x1": ((2, 10),),
     "x3": ((2, 11),),
-    "end": ((2, 9), (3, 15), (4, 6), (2, 12), (3, 10), (4, 8), (2, 13), (3, 11), (4, 12), (2, 14), (4, 10), (4, 9), (3, 13), (4, 11), (4, 14), (4, 13),),
+    "end": ((2, 9), (3, 8), (2, 12), (3, 15), (4, 6), (3, 10), (2, 13), (4, 8), (3, 11), (2, 14), (4, 9), (4, 12), (4, 10), (4, 11), (3, 13), (4, 14), (4, 13),),
 }
 MESH = pl.DeviceIdType.MESH
 f32 = jnp.float32
@@ -856,8 +856,7 @@
         ticks_at("x", blocks, b)
 
     loop(0, blocks, token_grad)
-    tick("end")
-    for u in range(len(units)):
+    def settle(u):
         core_copy(u).wait_send()
         for copy in across_copies(u):
             copy.wait_send()
@@ -881,8 +880,22 @@
             for k in range(1, nz):
                 along_copy(u, k).wait_send()
         out_copy(u).wait()
-    for b in range(blocks):
-        dx_copy(b).wait()
+
+    last = SCHEDULE["end"]
+    left = set(range(len(units)))
+    for k, (step, u) in enumerate(last):
+        if k == len(last) - 2:
+            for done in sorted(left - {v for _, v in last[k - 4 :]}):
+                settle(done)
+                left.remove(done)
+            for b in range(blocks):
+                dx_copy(b).wait()
+        if u == len(units):
+            vec_steps[step]()
+        else:
+            steps[step](u)
+    for u in sorted(left):
+        settle(u)
 
 
 def hand_over_kernel(count, *refs):

time: 134 us -> 133 us (level)
  no operation moved by 1% of the time
where the time goes in v4:
time: 133 us
  Pallas kernels  132 us (99%)
    pallas_call x1, Pallas kernels, fused_shards(): pl.pallas_call(partial(layer_kernel, n, rows, ff, names, len(small)), out...  127 us
    pallas_call x1, Pallas kernels, fused_shards(): pl.pallas_call(partial(hand_over_kernel, len(shapes)), out_shape=shapes,...  4.58 us

profile of v4, /device:TPU:0, one launch (start us, length us, event | category | flops | bytes accessed | tf_op | source)
XLA Modules:
  0.0 132.8 jit_solution(18363250729063058820)
XLA Ops:
  0.7 127.4 %shard_map.271 = (bf16[1024,768]{1,0:T(8,128)(2,1)}, f32[1,1]{1,0:T(1,128)}, bf16[1024,768]{1,0:T(8,128)(2,1)}, f32[48,2304]{1,0:T(8,128)}, f32[48,768]{1,0:T(8,...) custom-call(bf16[1024,768]{1,0:T(8,128)(2,1)} %bitcast.18, ...), custom_call_target="tpu_custom_call" | custom-call | tf_op jit(solution)/shard_map/pallas_call | solution.py:1015
  128.0 4.6 %shard_map.272 = (bf16[1024,768]{1,0:T(8,128)(2,1)}, f32[1,1]{1,0:T(1,128)}, bf16[1024,768]{1,0:T(8,128)(2,1)}, f32[48,2304]{1,0:T(8,128)}, f32[48,768]{1,0:T(8,...) custom-call(bf16[1024,768]{1,0:T(8,128)(2,1)} %get-tuple-element.45., ...), custom_call_target="tpu_custom_call" | custom-call | tf_op jit(solution)/shard_map/pallas_call | solution.py:1025
